TPU v7x, 128 devices: a whole 4x4x4 slice. The times are simulated.
128 devices in a mesh: pipe: 32 (over y, z, core), cross: 4 (over x).
Axes of the slice: x: 4, y: 4, z: 4, core: 2. Of those that a mesh axis runs over, the one named last changes fastest.
Arguments:
- state: float32 [5, 512, 9216], P(None, 'pipe', 'cross')
- face_diffusion: float32 [512, 9216], P('pipe', 'cross')
- courant: float32 [512, 9216], P('pipe', 'cross'), may hold values from -0.5 to 0.5
- cell_mask: int32 [512, 9216], P('pipe', 'cross'), may hold values from 0 to 1, as said below
- ghost_cell: int32 [16384], P(('pipe', 'cross')), may hold values from 0 to 36863, as said below
- ghost_owner: int32 [16384], P(('pipe', 'cross')), may hold values from 0 to 127, as said below
- ghost_image: int32 [16384], P(('pipe', 'cross')), may hold values from 0 to 255
- image_base: int32 [32768], P(('pipe', 'cross')), may hold values from 0 to 34462, as said below
- image_weight: float32 [8, 32768], P(None, ('pipe', 'cross')), may hold values from 0 to 0.25
Outputs:
- derivative: float32 [5, 512, 9216], P(None, 'pipe', 'cross')
- segment: float32 [5, 512, 9216], P(None, 'pipe', 'cross')
Inputs may be any that keep to these rules, and one draw needn't show every extreme that they name: `ghost_cell`: within one device's 128 entries the places are distinct, each a place of that device's block, and cell_mask is 1 at each of them. `ghost_owner`: A device number. Among one device's 128 ghost cells at most 2 name the same owner; one owner, the same for every device, is named by exactly 2 ghost cells of every device. `image_base`: the base row is at most 14, and the base pencil q has q + 97 inside the device's pencils and q + 1 on the same line of 96 pencils. `cell_mask`: 1 marks a solid cell.
All inputs are finite; a program needn't handle non-finite values.
Results may differ from a plain program's by a relative error of at most 0.0003.
Values sent between devices are 32-bit elements; how exact they have to be, the bound alone decides.
A program may use at most 128 MiB of HBM per device.

v0:
```python
import jax
import jax.numpy as jnp
from jax import lax
from jax.sharding import PartitionSpec as P

LINE = 96


REFLECT = (1.0, -1.0, -1.0, -1.0, 1.0)


def with_halo(x, sides, width):
    for axis, dim in sides:
        count, length = (lax.axis_size(axis), x.shape[dim])
        up = [(i, (i + 1) % count) for i in range(count - 1)]
        down = [(j, i) for i, j in up]
        last = lax.slice_in_dim(x, length - width, length, axis=dim)
        first = lax.slice_in_dim(x, 0, width, axis=dim)
        before = lax.ppermute(last, axis, up)
        after = lax.ppermute(first, axis, down)
        x = jnp.concatenate([before, x, after], axis=dim)
    return x


def passed_along(block, axis, distance):
    devices = range(lax.axis_size(axis))
    route = [(i - distance, i) for i in devices if i - distance in devices]
    return lax.ppermute(block, axis, route)


def corner_offsets(pencils):
    return jnp.array(
        [0, 1, LINE, LINE + 1, pencils, pencils + 1, pencils + LINE, pencils + LINE + 1], jnp.int32
    )


def combine(panels, lower_rows, upper_rows, has_lower, has_upper):
    lower_diag = jnp.where(has_lower, lower_rows[1], 1.0)
    upper_diag = jnp.where(has_upper, upper_rows[1], 1.0)
    lower_ratio = panels[0] / lower_diag
    upper_ratio = panels[2] / upper_diag
    new_lower = -lower_ratio * lower_rows[0]
    new_upper = -upper_ratio * upper_rows[2]
    new_margin = panels[3] - lower_ratio * lower_rows[3] - upper_ratio * upper_rows[3]
    new_diag = new_margin - new_lower - new_upper
    new_rhs = panels[4:] - lower_ratio * lower_rows[4:] - upper_ratio * upper_rows[4:]
    return jnp.concatenate(
        [jnp.stack([new_lower, new_diag, new_upper, new_margin]), new_rhs], axis=0
    )


def explicit_terms(padded, row_index, row_total):
    centre = padded[:, 2:-2]
    minus_one = padded[:, 1:-3]
    plus_one = padded[:, 3:-1]
    minus_two = padded[:, :-4]
    plus_two = padded[:, 4:]
    inner_terms = 7.0 / 9.0 * (plus_one - minus_one) + 1.0 / 36.0 * (plus_two - minus_two)
    near_terms = 0.75 * (plus_one - minus_one)
    first_terms = -1.5 * centre + 2.0 * plus_one - 0.5 * plus_two
    final_terms = 1.5 * centre - 2.0 * minus_one + 0.5 * minus_two
    edge_rows = (row_index == 1) | (row_index == row_total - 2)
    return jnp.where(
        row_index == 0,
        first_terms,
        jnp.where(
            row_index == row_total - 1, final_terms, jnp.where(edge_rows, near_terms, inner_terms)
        ),
    )


def derivative_panels(row_index, row_total, pencils, stencil_terms):
    edge_rows = (row_index == 1) | (row_index == row_total - 2)
    end_rows = (row_index == 0) | (row_index == row_total - 1)
    side_coef = jnp.where(end_rows, 0.0, jnp.where(edge_rows, 0.25, 1.0 / 3.0)) * jnp.ones(
        (1, pencils), jnp.float32
    )
    margin = 1.0 + side_coef + side_coef
    return jnp.concatenate(
        [jnp.stack([side_coef, jnp.ones_like(side_coef), side_coef, margin]), stencil_terms], axis=0
    )


def diffusion_panels(face_low, face_here, row_index, row_total, right_terms):
    lower_side = -face_low
    upper_side = -jnp.where(row_index == row_total - 1, 0.0, face_here)
    margin = jnp.ones_like(face_here)
    diagonal = margin - lower_side - upper_side
    return jnp.concatenate(
        [jnp.stack([lower_side, diagonal, upper_side, margin]), right_terms], axis=0
    )


def slab_solve(panels, row_index, row_total):
    row_count = panels.shape[1]
    stride = 1
    while stride < row_count:
        rimmed = with_halo(panels, (("pipe", 1),), stride)
        panels = combine(
            panels,
            rimmed[:, :row_count],
            rimmed[:, 2 * stride :],
            row_index >= stride,
            row_index < row_total - stride,
        )
        stride = stride * 2
    device_hops = 1
    while device_hops < lax.axis_size("pipe"):
        lower_rows = passed_along(panels, "pipe", device_hops)
        upper_rows = passed_along(panels, "pipe", -device_hops)
        stride = device_hops * row_count
        panels = combine(
            panels, lower_rows, upper_rows, row_index >= stride, row_index < row_total - stride
        )
        device_hops = device_hops * 2
    return panels[4:] / panels[1]


def local(
    state,
    face_diffusion,
    courant,
    cell_mask,
    ghost_cell,
    ghost_owner,
    ghost_image,
    image_base,
    image_weight,
):
    var_count, row_count, pencils = state.shape
    flat_state = state.reshape(var_count, row_count * pencils)
    corners = image_base[None, :] + corner_offsets(pencils)[:, None]
    image_values = jnp.sum(flat_state[:, corners] * image_weight[None], axis=1)
    images_here = image_values.shape[1]
    all_images = lax.all_gather(image_values, ("pipe", "cross"), axis=1, tiled=True)
    picked = all_images[:, ghost_owner * images_here + ghost_image]
    reflection = jnp.array(REFLECT, jnp.float32)[:, None]
    cleared = jnp.where(cell_mask.reshape(1, -1) == 1, 0.0, flat_state)
    filled = (
        cleared.at[:, ghost_cell].set(reflection * picked).reshape(var_count, row_count, pencils)
    )
    stacked = jnp.concatenate([filled, face_diffusion[None]], axis=0)
    rimmed = with_halo(stacked, (("pipe", 1),), 2)
    row_total = row_count * lax.axis_size("pipe")
    row_index = lax.axis_index("pipe") * row_count + lax.broadcasted_iota(
        jnp.int32, (row_count, 1), 0
    )
    stencil_terms = explicit_terms(rimmed[:var_count], row_index, row_total)
    face_low = rimmed[var_count, 1:-3]
    derivative = slab_solve(
        derivative_panels(row_index, row_total, pencils, stencil_terms), row_index, row_total
    )
    rhs_two = filled - courant[None] * derivative
    segment = slab_solve(
        diffusion_panels(face_low, face_diffusion, row_index, row_total, rhs_two),
        row_index,
        row_total,
    )
    return (derivative, segment)


def solution(mesh):
    in_specs = (
        P(None, "pipe", "cross"),
        P("pipe", "cross"),
        P("pipe", "cross"),
        P("pipe", "cross"),
        P(("pipe", "cross")),
        P(("pipe", "cross")),
        P(("pipe", "cross")),
        P(("pipe", "cross")),
        P(None, ("pipe", "cross")),
    )
    out_specs = (P(None, "pipe", "cross"), P(None, "pipe", "cross"))
    return jax.shard_map(local, mesh=mesh, in_specs=in_specs, out_specs=out_specs, check_vma=False)
```

profile of v0, /device:TPU:1, one launch (start us, length us, event | category | flops | bytes accessed | tf_op | source)
XLA Modules:
  0.0 691.1 jit_solution(11439552856497325618)
XLA Ops:
  1.7 10.7 %copy.18 = f32[5,16,2304]{0,2,1:T(8,128)} copy(f32[5,16,2304]{2,1,0:T(8,128)} %param.11) | data formatting | bytes 1474560 | tf_op args[0]
  12.5 21.1 %broadcast_select_fusion = f32[5,36864]{0,1:T(8,128)} fusion(pred[36864]{0:T(1024)(128)(4,1)S(1)} %eq.64, f32[5,16,2304]{0,2,1:T(8,128)} %copy.18), kind=kLoop, calls=%fused_computation.3 | loop fusion | flops 184320 | bytes 1511424 | tf_op jit(solution)/shard_map/jit(_where)/select_n | solution.py:138
  33.6 11.8 %gather_fusion = f32[2048,5]{1,0:T(8,128)S(1)} fusion(f32[5,36864]{0,1:T(8,128)} %bitcast.515, s32[2048]{0:T(1024)S(1)} %broadcast_clamp_fusion), kind=kCustom, calls=%fused_computation | custom fusion | bytes 90112 | tf_op jit(solution)/shard_map/gather | solution.py:133
  45.8 108.0 %all_gather.3 = f32[5,32768]{0,1:T(8,128)} all-gather(f32[5,256]{0,1:T(8,128)S(1)} %bitcast.539), channel_id=1, replica_groups=mesh['pipe'=32,'cross'=4] {'pipe','cross'}, dimensions={1}, use_global_device_ids=true | all-gather | bytes 660480 | tf_op jit(solution)/shard_map/all_gather | solution.py:135
  153.9 14.8 %scatter_custom_fusion = f32[5,36864]{0,1:T(8,128)} fusion(f32[5,36864]{0,1:T(8,128)} %broadcast_select_fusion, s32[128]{0:T(128)S(1)} %compare_select_fusion.2, f32[5]{0:T(128)S(1)} %copy-done.5, f32[5,32768]{0,1:T(8,128)} %all_gather.3, s32[1024]{0:T(1024)S(1)} %pad_clamp_fusion), kind=kCustom, calls=%fused_computation.556 | custom fusion | flops 640 | bytes 17519104 | tf_op jit(solution)/shard_map/scatter | solution.py:140
  168.6 11.1 %copy.19 = f32[5,16,2304]{2,1,0:T(8,128)S(1)} copy(f32[5,16,2304]{0,2,1:T(8,128)} %bitcast.516) | data formatting | bytes 1474560 | tf_op jit(solution)/shard_map/reshape | solution.py:140
  181.8 4.3 collective-permute-start
  193.7 3.2 collective-permute-done.3
  202.5 4.6 collective-permute-done.5
  209.8 2.4 collective-permute-start.7
  214.1 9.1 %collective-permute-done.7 = f32[9,4,2304]{2,1,0:T(4,128)S(1)} collective-permute-done((f32[9,4,2304]{2,1,0:T(4,128)S(1)}, f32[9,4,2304]{2,1,0:T(4,128)S(1)}, u32[]{:S(2)}, u32[]{:S(2)}) %collective-permute-start.7) | collective-permute-done | bytes 331808 | tf_op jit(solution)/shard_map/ppermute | solution.py:20
  225.8 2.4 collective-permute-start.9
  228.6 4.8 collective-permute-done.8
  233.6 5.7 collective-permute-done.9
  241.9 2.5 collective-permute-start.11
  244.4 12.2 %collective-permute-done.10 = f32[9,16,2304]{2,1,0:T(8,128)S(1)} collective-permute-done((f32[9,16,2304]{2,1,0:T(8,128)S(1)}, f32[9,16,2304]{2,1,0:T(8,128)S(1)}, u32[]{:S(2)}, u32[]{:S(2)}) %collective-permute-start.10) | collective-permute-done | bytes 1327136 | tf_op jit(solution)/shard_map/ppermute | solution.py:28
  256.7 6.4 collective-permute-done.11
  263.5 5.4 collective-permute-start.12
  270.4 24.3 %collective-permute-done.12 = f32[9,16,2304]{2,1,0:T(8,128)S(1)} collective-permute-done((f32[9,16,2304]{2,1,0:T(8,128)S(1)}, f32[9,16,2304]{2,1,0:T(8,128)S(1)}, u32[]{:S(2)}, u32[]{:S(2)}) %collective-permute-start.12) | collective-permute-done | bytes 1327136 | tf_op jit(solution)/shard_map/ppermute | solution.py:28
  294.8 5.7 collective-permute-done.13
  300.9 9.2 %collective-permute-start.14 = (f32[9,16,2304]{2,1,0:T(8,128)S(1)}, f32[9,16,2304]{2,1,0:T(8,128)S(1)}, u32[]{:S(2)}, u32[]{:S(2)}) collective-permute-start(f32[9,16,2304]{2,1,0:T(8,128)S(1)} %get-tuple-element.98), channel_id=1, source_target_pairs={{0,16},{4,20},{8,24},{12,28},{16,32},{20,36},{24,40},{28,44},{32,4... | collective-permute-start | bytes 3981320 | tf_op jit(solution)/shard_map/ppermute | solution.py:28
  311.5 55.9 %collective-permute-done.14 = f32[9,16,2304]{2,1,0:T(8,128)S(1)} collective-permute-done((f32[9,16,2304]{2,1,0:T(8,128)S(1)}, f32[9,16,2304]{2,1,0:T(8,128)S(1)}, u32[]{:S(2)}, u32[]{:S(2)}) %collective-permute-start.14) | collective-permute-done | bytes 1327136 | tf_op jit(solution)/shard_map/ppermute | solution.py:28
  367.8 5.1 collective-permute-start.16
  374.2 26.6 %collective-permute-done.16 = f32[9,16,2304]{2,1,0:T(8,128)S(1)} collective-permute-done((f32[9,16,2304]{2,1,0:T(8,128)S(1)}, f32[9,16,2304]{2,1,0:T(8,128)S(1)}, u32[]{:S(2)}, u32[]{:S(2)}) %collective-permute-start.16) | collective-permute-done | bytes 1327136 | tf_op jit(solution)/shard_map/ppermute | solution.py:28
  400.9 3.8 collective-permute-done.17
  406.4 5.7 collective-permute-start.18
  412.2 25.3 %collective-permute-done.19 = f32[9,16,2304]{2,1,0:T(8,128)S(1)} collective-permute-done((f32[9,16,2304]{2,1,0:T(8,128)S(1)}, f32[9,16,2304]{2,1,0:T(8,128)S(1)}, u32[]{:S(2)}, u32[]{:S(2)}) %collective-permute-start.19) | collective-permute-done | bytes 1327136 | tf_op jit(solution)/shard_map/ppermute | solution.py:28
  439.0 5.5 collective-permute-start.20
  446.6 3.7 collective-permute-done.21
  455.6 4.1 collective-permute-done.23
  466.4 4.3 collective-permute-done.25
  473.3 2.4 collective-permute-start.27
  475.7 5.1 collective-permute-done.26
  481.0 5.1 collective-permute-done.27
  488.4 2.5 collective-permute-start.29
  490.9 12.2 %collective-permute-done.28 = f32[9,16,2304]{2,1,0:T(8,128)S(1)} collective-permute-done((f32[9,16,2304]{2,1,0:T(8,128)S(1)}, f32[9,16,2304]{2,1,0:T(8,128)S(1)}, u32[]{:S(2)}, u32[]{:S(2)}) %collective-permute-start.28) | collective-permute-done | bytes 1327136 | tf_op jit(solution)/shard_map/ppermute | solution.py:28
  503.2 6.4 collective-permute-done.29
  510.0 5.4 collective-permute-start.30
  516.8 24.5 %collective-permute-done.30 = f32[9,16,2304]{2,1,0:T(8,128)S(1)} collective-permute-done((f32[9,16,2304]{2,1,0:T(8,128)S(1)}, f32[9,16,2304]{2,1,0:T(8,128)S(1)}, u32[]{:S(2)}, u32[]{:S(2)}) %collective-permute-start.30) | collective-permute-done | bytes 1327136 | tf_op jit(solution)/shard_map/ppermute | solution.py:28
  541.4 5.7 collective-permute-done.31
  547.5 9.2 %collective-permute-start.32 = (f32[9,16,2304]{2,1,0:T(8,128)S(1)}, f32[9,16,2304]{2,1,0:T(8,128)S(1)}, u32[]{:S(2)}, u32[]{:S(2)}) collective-permute-start(f32[9,16,2304]{2,1,0:T(8,128)S(1)} %get-tuple-element.20), channel_id=1, source_target_pairs={{0,16},{4,20},{8,24},{12,28},{16,32},{20,36},{24,40},{28,44},{32,4... | collective-permute-start | bytes 3981320 | tf_op jit(solution)/shard_map/ppermute | solution.py:28
  558.1 55.9 %collective-permute-done.32 = f32[9,16,2304]{2,1,0:T(8,128)S(1)} collective-permute-done((f32[9,16,2304]{2,1,0:T(8,128)S(1)}, f32[9,16,2304]{2,1,0:T(8,128)S(1)}, u32[]{:S(2)}, u32[]{:S(2)}) %collective-permute-start.32) | collective-permute-done | bytes 1327136 | tf_op jit(solution)/shard_map/ppermute | solution.py:28
  614.5 5.1 collective-permute-start.34
  620.8 26.7 %collective-permute-done.34 = f32[9,16,2304]{2,1,0:T(8,128)S(1)} collective-permute-done((f32[9,16,2304]{2,1,0:T(8,128)S(1)}, f32[9,16,2304]{2,1,0:T(8,128)S(1)}, u32[]{:S(2)}, u32[]{:S(2)}) %collective-permute-start.34) | collective-permute-done | bytes 1327136 | tf_op jit(solution)/shard_map/ppermute | solution.py:28
  647.6 5.5 collective-permute-done.35
  653.5 4.3 collective-permute-start.36
  659.1 25.4 %collective-permute-done.36 = f32[9,16,2304]{2,1,0:T(8,128)S(1)} collective-permute-done((f32[9,16,2304]{2,1,0:T(8,128)S(1)}, f32[9,16,2304]{2,1,0:T(8,128)S(1)}, u32[]{:S(2)}, u32[]{:S(2)}) %collective-permute-start.36) | collective-permute-done | bytes 1327136 | tf_op jit(solution)/shard_map/ppermute | solution.py:28
  684.6 5.3 collective-permute-done.37
  (196 shorter events, 62.6 us)
Async XLA Ops:
  1.7 10.7 %copy-start.7 = (s32[128]{0:T(128)S(1)}, s32[128]{0:T(128)}, u32[]{:S(2)}) copy-start(s32[128]{0:T(128)} %param.15) | copy-start | bytes 1540
  1.7 10.7 %copy-start.4 = (s32[256]{0:T(256)S(1)}, s32[256]{0:T(256)}, u32[]{:S(2)}) copy-start(s32[256]{0:T(256)} %param.18) | copy-start | bytes 3076
  1.7 10.7 %copy-start.6 = (s32[8]{0:T(128)S(1)}, s32[8]{0:T(128)}, u32[]{:S(2)}) copy-start(s32[8]{0:T(128)} %constant.29.clone) | copy-start | bytes 100
  12.5 32.9 %copy-start.3 = (f32[8,256]{1,0:T(8,128)S(1)}, f32[8,256]{1,0:T(8,128)}, u32[]{:S(2)}) copy-start(f32[8,256]{1,0:T(8,128)} %param.19) | copy-start | bytes 24580
  45.8 108.0 %copy-start.8 = (s32[128]{0:T(128)S(1)}, s32[128]{0:T(128)}, u32[]{:S(2)}) copy-start(s32[128]{0:T(128)} %param.17) | copy-start | bytes 1540
  45.8 108.0 %copy-start.9 = (s32[128]{0:T(128)S(1)}, s32[128]{0:T(128)}, u32[]{:S(2)}) copy-start(s32[128]{0:T(128)} %param.16) | copy-start | bytes 1540
  45.8 108.0 %copy-start.5 = (f32[5]{0:T(128)S(1)}, f32[5]{0:T(128)}, u32[]{:S(2)}) copy-start(f32[5]{0:T(128)} %constant.30.clone) | copy-start | bytes 64
  168.6 11.1 %copy-start = (f32[16,2304]{1,0:T(8,128)S(1)}, f32[16,2304]{1,0:T(8,128)}, u32[]{:S(2)}) copy-start(f32[16,2304]{1,0:T(8,128)} %param.12) | copy-start | bytes 442372
  179.8 6.7 collective-permute-start.1
  181.8 6.2 collective-permute-start
  188.9 4.6 collective-permute-start.2
  191.2 5.8 collective-permute-start.3
  197.7 4.6 collective-permute-start.4
  199.9 7.3 %collective-permute-start.5 = (f32[9,2,2304]{2,1,0:T(2,128)S(1)}, f32[9,2,2304]{2,1,0:T(2,128)S(1)}, u32[]{:S(2)}, u32[]{:S(2)}) collective-permute-start(f32[9,2,2304]{2,1,0:T(2,128)S(1)} %get-tuple-element.179), channel_id=1, source_target_pairs={{4,0},{8,4},{12,8},{16,12},{20,16},{24,20},{28,24},{32,28},{36,32}... | collective-permute-start | bytes 497672 | tf_op jit(solution)/shard_map/ppermute | solution.py:20
  207.9 6.0 collective-permute-start.6
  209.8 13.4 %collective-permute-start.7 = (f32[9,4,2304]{2,1,0:T(4,128)S(1)}, f32[9,4,2304]{2,1,0:T(4,128)S(1)}, u32[]{:S(2)}, u32[]{:S(2)}) collective-permute-start(f32[9,4,2304]{2,1,0:T(4,128)S(1)} %get-tuple-element.175), channel_id=1, source_target_pairs={{4,0},{8,4},{12,8},{16,12},{20,16},{24,20},{28,24},{32,28},{36,32}... | collective-permute-start | bytes 995336 | tf_op jit(solution)/shard_map/ppermute | solution.py:20
  223.9 9.5 %collective-permute-start.8 = (f32[9,8,2304]{2,1,0:T(8,128)S(1)}, f32[9,8,2304]{2,1,0:T(8,128)S(1)}, u32[]{:S(2)}, u32[]{:S(2)}) collective-permute-start(f32[9,8,2304]{2,1,0:T(8,128)S(1)} %get-tuple-element.172), channel_id=1, source_target_pairs={{0,4},{4,8},{8,12},{12,16},{16,20},{20,24},{24,28},{28,32},{32,36}... | collective-permute-start | bytes 1990664 | tf_op jit(solution)/shard_map/ppermute | solution.py:19
  225.8 13.5 %collective-permute-start.9 = (f32[9,8,2304]{2,1,0:T(8,128)S(1)}, f32[9,8,2304]{2,1,0:T(8,128)S(1)}, u32[]{:S(2)}, u32[]{:S(2)}) collective-permute-start(f32[9,8,2304]{2,1,0:T(8,128)S(1)} %get-tuple-element.171), channel_id=1, source_target_pairs={{4,0},{8,4},{12,8},{16,12},{20,16},{24,20},{28,24},{32,28},{36,32}... | collective-permute-start | bytes 1990664 | tf_op jit(solution)/shard_map/ppermute | solution.py:20
  239.9 16.6 %collective-permute-start.10 = (f32[9,16,2304]{2,1,0:T(8,128)S(1)}, f32[9,16,2304]{2,1,0:T(8,128)S(1)}, u32[]{:S(2)}, u32[]{:S(2)}) collective-permute-start(f32[9,16,2304]{2,1,0:T(8,128)S(1)} %get-tuple-element.112), channel_id=1, source_target_pairs={{0,4},{4,8},{8,12},{12,16},{16,20},{20,24},{24,28},{28,32},{32,36}... | collective-permute-start | bytes 3981320 | tf_op jit(solution)/shard_map/ppermute | solution.py:28
  241.9 21.2 %collective-permute-start.11 = (f32[9,16,2304]{2,1,0:T(8,128)S(1)}, f32[9,16,2304]{2,1,0:T(8,128)S(1)}, u32[]{:S(2)}, u32[]{:S(2)}) collective-permute-start(f32[9,16,2304]{2,1,0:T(8,128)S(1)} %get-tuple-element.112), channel_id=1, source_target_pairs={{4,0},{8,4},{12,8},{16,12},{20,16},{24,20},{28,24},{32,28},{36,32}... | collective-permute-start | bytes 3981320 | tf_op jit(solution)/shard_map/ppermute | solution.py:28
  263.5 31.3 %collective-permute-start.12 = (f32[9,16,2304]{2,1,0:T(8,128)S(1)}, f32[9,16,2304]{2,1,0:T(8,128)S(1)}, u32[]{:S(2)}, u32[]{:S(2)}) collective-permute-start(f32[9,16,2304]{2,1,0:T(8,128)S(1)} %get-tuple-element.105), channel_id=1, source_target_pairs={{0,8},{4,12},{8,16},{12,20},{16,24},{20,28},{24,32},{28,36},{32,40... | collective-permute-start | bytes 3981320 | tf_op jit(solution)/shard_map/ppermute | solution.py:28
  268.9 31.6 %collective-permute-start.13 = (f32[9,16,2304]{2,1,0:T(8,128)S(1)}, f32[9,16,2304]{2,1,0:T(8,128)S(1)}, u32[]{:S(2)}, u32[]{:S(2)}) collective-permute-start(f32[9,16,2304]{2,1,0:T(8,128)S(1)} %get-tuple-element.105), channel_id=1, source_target_pairs={{8,0},{12,4},{16,8},{20,12},{24,16},{28,20},{32,24},{36,28},{40,32... | collective-permute-start | bytes 3981320 | tf_op jit(solution)/shard_map/ppermute | solution.py:28
  300.9 66.4 %collective-permute-start.14 = (f32[9,16,2304]{2,1,0:T(8,128)S(1)}, f32[9,16,2304]{2,1,0:T(8,128)S(1)}, u32[]{:S(2)}, u32[]{:S(2)}) collective-permute-start(f32[9,16,2304]{2,1,0:T(8,128)S(1)} %get-tuple-element.98), channel_id=1, source_target_pairs={{0,16},{4,20},{8,24},{12,28},{16,32},{20,36},{24,40},{28,44},{32,4... | collective-permute-start | bytes 3981320 | tf_op jit(solution)/shard_map/ppermute | solution.py:28
  310.1 57.3 %collective-permute-start.15 = (f32[9,16,2304]{2,1,0:T(8,128)S(1)}, f32[9,16,2304]{2,1,0:T(8,128)S(1)}, u32[]{:S(2)}, u32[]{:S(2)}) collective-permute-start(f32[9,16,2304]{2,1,0:T(8,128)S(1)} %get-tuple-element.98), channel_id=1, source_target_pairs={{16,0},{20,4},{24,8},{28,12},{32,16},{36,20},{40,24},{44,28},{48,3... | collective-permute-start | bytes 3981320 | tf_op jit(solution)/shard_map/ppermute | solution.py:28
  367.8 33.0 %collective-permute-start.16 = (f32[9,16,2304]{2,1,0:T(8,128)S(1)}, f32[9,16,2304]{2,1,0:T(8,128)S(1)}, u32[]{:S(2)}, u32[]{:S(2)}) collective-permute-start(f32[9,16,2304]{2,1,0:T(8,128)S(1)} %get-tuple-element.91), channel_id=1, source_target_pairs={{0,32},{4,36},{8,40},{12,44},{16,48},{20,52},{24,56},{28,60},{32,6... | collective-permute-start | bytes 3981320 | tf_op jit(solution)/shard_map/ppermute | solution.py:28
  372.9 31.9 %collective-permute-start.17 = (f32[9,16,2304]{2,1,0:T(8,128)S(1)}, f32[9,16,2304]{2,1,0:T(8,128)S(1)}, u32[]{:S(2)}, u32[]{:S(2)}) collective-permute-start(f32[9,16,2304]{2,1,0:T(8,128)S(1)} %get-tuple-element.91), channel_id=1, source_target_pairs={{32,0},{36,4},{40,8},{44,12},{48,16},{52,20},{56,24},{60,28},{64,3... | collective-permute-start | bytes 3981320 | tf_op jit(solution)/shard_map/ppermute | solution.py:28
  405.1 32.4 %collective-permute-start.19 = (f32[9,16,2304]{2,1,0:T(8,128)S(1)}, f32[9,16,2304]{2,1,0:T(8,128)S(1)}, u32[]{:S(2)}, u32[]{:S(2)}) collective-permute-start(f32[9,16,2304]{2,1,0:T(8,128)S(1)} %get-tuple-element.84), channel_id=1, source_target_pairs={{64,0},{68,4},{72,8},{76,12},{80,16},{84,20},{88,24},{92,28},{96,3... | collective-permute-start | bytes 3981320 | tf_op jit(solution)/shard_map/ppermute | solution.py:28
  406.4 32.1 %collective-permute-start.18 = (f32[9,16,2304]{2,1,0:T(8,128)S(1)}, f32[9,16,2304]{2,1,0:T(8,128)S(1)}, u32[]{:S(2)}, u32[]{:S(2)}) collective-permute-start(f32[9,16,2304]{2,1,0:T(8,128)S(1)} %get-tuple-element.84), channel_id=1, source_target_pairs={{0,64},{4,68},{8,72},{12,76},{16,80},{20,84},{24,88},{28,92},{32,9... | collective-permute-start | bytes 3981320 | tf_op jit(solution)/shard_map/ppermute | solution.py:28
  412.1 26.5 %copy-start.2 = (f32[16,2304]{1,0:T(8,128)S(1)}, f32[16,2304]{1,0:T(8,128)}, u32[]{:S(2)}) copy-start(f32[16,2304]{1,0:T(8,128)} %param.13) | copy-start | bytes 442372
  438.9 11.7 %copy-start.1 = (f32[5,16,2304]{2,1,0:T(8,128)}, f32[5,16,2304]{2,1,0:T(8,128)S(1)}, u32[]{:S(2)}) copy-start(f32[5,16,2304]{2,1,0:T(8,128)S(1)} %get-tuple-element.78) | copy-start | bytes 2211844
  439.0 7.4 %collective-permute-start.20 = (f32[9,1,2304]{2,1,0:T(1,128)S(1)}, f32[9,1,2304]{2,1,0:T(1,128)S(1)}, u32[]{:S(2)}, u32[]{:S(2)}) collective-permute-start(f32[9,1,2304]{2,1,0:T(1,128)S(1)} %get-tuple-element.168), channel_id=1, source_target_pairs={{0,4},{4,8},{8,12},{12,16},{16,20},{20,24},{24,28},{28,32},{32,36}... | collective-permute-start | bytes 248840 | tf_op jit(solution)/shard_map/ppermute | solution.py:19
  444.5 5.8 collective-permute-start.21
  451.1 4.4 collective-permute-start.22
  453.0 6.7 collective-permute-start.23
  460.4 6.0 collective-permute-start.24
  462.3 8.4 %collective-permute-start.25 = (f32[9,4,2304]{2,1,0:T(4,128)S(1)}, f32[9,4,2304]{2,1,0:T(4,128)S(1)}, u32[]{:S(2)}, u32[]{:S(2)}) collective-permute-start(f32[9,4,2304]{2,1,0:T(4,128)S(1)} %get-tuple-element.163), channel_id=1, source_target_pairs={{4,0},{8,4},{12,8},{16,12},{20,16},{24,20},{28,24},{32,28},{36,32}... | collective-permute-start | bytes 995336 | tf_op jit(solution)/shard_map/ppermute | solution.py:20
  471.3 9.5 %collective-permute-start.26 = (f32[9,8,2304]{2,1,0:T(8,128)S(1)}, f32[9,8,2304]{2,1,0:T(8,128)S(1)}, u32[]{:S(2)}, u32[]{:S(2)}) collective-permute-start(f32[9,8,2304]{2,1,0:T(8,128)S(1)} %get-tuple-element.162), channel_id=1, source_target_pairs={{0,4},{4,8},{8,12},{12,16},{16,20},{20,24},{24,28},{28,32},{32,36}... | collective-permute-start | bytes 1990664 | tf_op jit(solution)/shard_map/ppermute | solution.py:19
  473.3 12.8 %collective-permute-start.27 = (f32[9,8,2304]{2,1,0:T(8,128)S(1)}, f32[9,8,2304]{2,1,0:T(8,128)S(1)}, u32[]{:S(2)}, u32[]{:S(2)}) collective-permute-start(f32[9,8,2304]{2,1,0:T(8,128)S(1)} %get-tuple-element.161), channel_id=1, source_target_pairs={{4,0},{8,4},{12,8},{16,12},{20,16},{24,20},{28,24},{32,28},{36,32}... | collective-permute-start | bytes 1990664 | tf_op jit(solution)/shard_map/ppermute | solution.py:20
  486.5 16.6 %collective-permute-start.28 = (f32[9,16,2304]{2,1,0:T(8,128)S(1)}, f32[9,16,2304]{2,1,0:T(8,128)S(1)}, u32[]{:S(2)}, u32[]{:S(2)}) collective-permute-start(f32[9,16,2304]{2,1,0:T(8,128)S(1)} %get-tuple-element.36), channel_id=1, source_target_pairs={{0,4},{4,8},{8,12},{12,16},{16,20},{20,24},{24,28},{28,32},{32,36}... | collective-permute-start | bytes 3981320 | tf_op jit(solution)/shard_map/ppermute | solution.py:28
  488.4 21.2 %collective-permute-start.29 = (f32[9,16,2304]{2,1,0:T(8,128)S(1)}, f32[9,16,2304]{2,1,0:T(8,128)S(1)}, u32[]{:S(2)}, u32[]{:S(2)}) collective-permute-start(f32[9,16,2304]{2,1,0:T(8,128)S(1)} %get-tuple-element.36), channel_id=1, source_target_pairs={{4,0},{8,4},{12,8},{16,12},{20,16},{24,20},{28,24},{32,28},{36,32}... | collective-permute-start | bytes 3981320 | tf_op jit(solution)/shard_map/ppermute | solution.py:28
  510.0 31.3 %collective-permute-start.30 = (f32[9,16,2304]{2,1,0:T(8,128)S(1)}, f32[9,16,2304]{2,1,0:T(8,128)S(1)}, u32[]{:S(2)}, u32[]{:S(2)}) collective-permute-start(f32[9,16,2304]{2,1,0:T(8,128)S(1)} %get-tuple-element.28), channel_id=1, source_target_pairs={{0,8},{4,12},{8,16},{12,20},{16,24},{20,28},{24,32},{28,36},{32,40... | collective-permute-start | bytes 3981320 | tf_op jit(solution)/shard_map/ppermute | solution.py:28
  515.5 31.6 %collective-permute-start.31 = (f32[9,16,2304]{2,1,0:T(8,128)S(1)}, f32[9,16,2304]{2,1,0:T(8,128)S(1)}, u32[]{:S(2)}, u32[]{:S(2)}) collective-permute-start(f32[9,16,2304]{2,1,0:T(8,128)S(1)} %get-tuple-element.28), channel_id=1, source_target_pairs={{8,0},{12,4},{16,8},{20,12},{24,16},{28,20},{32,24},{36,28},{40,32... | collective-permute-start | bytes 3981320 | tf_op jit(solution)/shard_map/ppermute | solution.py:28
  547.5 66.4 %collective-permute-start.32 = (f32[9,16,2304]{2,1,0:T(8,128)S(1)}, f32[9,16,2304]{2,1,0:T(8,128)S(1)}, u32[]{:S(2)}, u32[]{:S(2)}) collective-permute-start(f32[9,16,2304]{2,1,0:T(8,128)S(1)} %get-tuple-element.20), channel_id=1, source_target_pairs={{0,16},{4,20},{8,24},{12,28},{16,32},{20,36},{24,40},{28,44},{32,4... | collective-permute-start | bytes 3981320 | tf_op jit(solution)/shard_map/ppermute | solution.py:28
  556.8 57.3 %collective-permute-start.33 = (f32[9,16,2304]{2,1,0:T(8,128)S(1)}, f32[9,16,2304]{2,1,0:T(8,128)S(1)}, u32[]{:S(2)}, u32[]{:S(2)}) collective-permute-start(f32[9,16,2304]{2,1,0:T(8,128)S(1)} %get-tuple-element.20), channel_id=1, source_target_pairs={{16,0},{20,4},{24,8},{28,12},{32,16},{36,20},{40,24},{44,28},{48,3... | collective-permute-start | bytes 3981320 | tf_op jit(solution)/shard_map/ppermute | solution.py:28
  614.5 33.0 %collective-permute-start.34 = (f32[9,16,2304]{2,1,0:T(8,128)S(1)}, f32[9,16,2304]{2,1,0:T(8,128)S(1)}, u32[]{:S(2)}, u32[]{:S(2)}) collective-permute-start(f32[9,16,2304]{2,1,0:T(8,128)S(1)} %get-tuple-element.12), channel_id=1, source_target_pairs={{0,32},{4,36},{8,40},{12,44},{16,48},{20,52},{24,56},{28,60},{32,6... | collective-permute-start | bytes 3981320 | tf_op jit(solution)/shard_map/ppermute | solution.py:28
  619.5 33.6 %collective-permute-start.35 = (f32[9,16,2304]{2,1,0:T(8,128)S(1)}, f32[9,16,2304]{2,1,0:T(8,128)S(1)}, u32[]{:S(2)}, u32[]{:S(2)}) collective-permute-start(f32[9,16,2304]{2,1,0:T(8,128)S(1)} %get-tuple-element.12), channel_id=1, source_target_pairs={{32,0},{36,4},{40,8},{44,12},{48,16},{52,20},{56,24},{60,28},{64,3... | collective-permute-start | bytes 3981320 | tf_op jit(solution)/shard_map/ppermute | solution.py:28
  653.5 31.0 %collective-permute-start.36 = (f32[9,16,2304]{2,1,0:T(8,128)S(1)}, f32[9,16,2304]{2,1,0:T(8,128)S(1)}, u32[]{:S(2)}, u32[]{:S(2)}) collective-permute-start(f32[9,16,2304]{2,1,0:T(8,128)S(1)} %get-tuple-element.4), channel_id=1, source_target_pairs={{0,64},{4,68},{8,72},{12,76},{16,80},{20,84},{24,88},{28,92},{32,9... | collective-permute-start | bytes 3981320 | tf_op jit(solution)/shard_map/ppermute | solution.py:28
  657.8 32.1 %collective-permute-start.37 = (f32[9,16,2304]{2,1,0:T(8,128)S(1)}, f32[9,16,2304]{2,1,0:T(8,128)S(1)}, u32[]{:S(2)}, u32[]{:S(2)}) collective-permute-start(f32[9,16,2304]{2,1,0:T(8,128)S(1)} %get-tuple-element.4), channel_id=1, source_target_pairs={{64,0},{68,4},{72,8},{76,12},{80,16},{84,20},{88,24},{92,28},{96,3... | collective-permute-start | bytes 3981320 | tf_op jit(solution)/shard_map/ppermute | solution.py:28
where the time goes:
time: 694 us; the launch traced here: 691 us
  waiting for transfers between devices  383 us (55%)
  starting transfers between devices  113 us (16%)
  blocking collectives  108 us (16%)
  other arithmetic  49 us (7%)
  local copies, waits for them, and re-layouts  36.3 us (5%)
    ppermute x20, waiting for transfers between devices, passed_along(): return lax.ppermute(block, axis, route)  329 us
    all_gather x1, blocking collectives, local(): lax.all_gather(image_values, ('pipe', 'cross'), axis=1, tiled=True)  108 us
    ppermute x20, starting transfers between devices, passed_along(): return lax.ppermute(block, axis, route)  68.8 us
    ppermute x9, waiting for transfers between devices, with_halo(): after = lax.ppermute(first, axis, down)  41.5 us
    ppermute x9, starting transfers between devices, with_halo(): after = lax.ppermute(first, axis, down)  23.2 us
    select_n x1, other arithmetic, local(): cleared = jnp.where(cell_mask.reshape(1, -1) == 1, 0.0, flat_state)  21.1 us
    ppermute x9, starting transfers between devices, with_halo(): before = lax.ppermute(last, axis, up)  20.9 us
    scatter x1, other arithmetic, local(): cleared.at[:, ghost_cell].set(reflection * picked)  14.8 us
  transfers between devices with their start and end apart: 38, of which 31 were waited for; matrix products, arithmetic and copies ran while one was open for 1% of the time, Pallas kernels for 0%

commit v1 on v0

v1 whole, which is shorter than its diff:
```python
import functools

import jax
import jax.numpy as jnp
import numpy as np
from jax import lax
from jax.experimental import pallas as pl
from jax.experimental.pallas import tpu as pltpu
from jax.sharding import PartitionSpec as P

VARS = 5
ROWS = 16
GHOSTS = 128
IMAGES = 256
UNITS = 3
REFLECT = (1.0, -1.0, -1.0, -1.0, 1.0)
F32 = jnp.float32
I32 = jnp.int32
MESH = pl.DeviceIdType.MESH

T_R = 0
T_S = 17
T_K = 34
T_U = 52
T_V = 68
T_H0 = 84
T_H1 = 87
T_H14 = 91
T_H15 = 95
T_D0, T_D15, T_DL, T_DR = 98, 99, 100, 101


def derivative_constants(slabs):
    n = slabs * ROWS
    side = np.full(n, 1.0 / 3.0)
    side[1] = side[n - 2] = 0.25
    side[0] = side[n - 1] = 0.0
    delta, eps = np.ones(n), np.ones(n)
    for k in range(n - 2, -1, -1):
        delta[k] = 1.0 - side[k] * side[k + 1] / delta[k + 1]
    for k in range(1, n):
        eps[k] = 1.0 - side[k] * side[k - 1] / eps[k - 1]
    r, s, e = -side / delta, -side / eps, 1.0 / (delta + eps - 1.0)

    def at(x, i):
        return x[i] if 0 <= i < n else 0.0

    table = np.zeros((slabs, 128))
    decay_l, decay_r = np.zeros(slabs), np.zeros(slabs)
    for p in range(slabs):
        g = p * ROWS
        row = table[p]
        kappa = {k: 25.0 / 36.0 * at(e, g + k) for k in range(-1, ROWS + 1)}
        for k in range(0, ROWS + 1):
            row[T_R + k] = at(r, g + k)
        for k in range(-1, ROWS):
            row[T_S + k + 1] = at(s, g + k)
        for k in range(-1, ROWS + 1):
            row[T_K + k + 1] = kappa[k]
        u = v = 1.0
        for k in range(ROWS):
            u = u * at(r, g + k) if k else 1.0
            row[T_U + k] = u
        for k in range(ROWS - 1, -1, -1):
            v = v * at(s, g + k) if k < ROWS - 1 else 1.0
            row[T_V + k] = v
        decay_l[p] = u * at(r, g + ROWS)
        decay_r[p] = v * at(s, g - 1)
        row[T_H0 : T_H0 + 3] = (0.0, kappa[0], 0.0)
        row[T_H1 : T_H1 + 4] = (-kappa[1], 0.0, kappa[1], 0.0)
        row[T_H14 : T_H14 + 4] = (0.0, -kappa[14], 0.0, kappa[14])
        row[T_H15 : T_H15 + 3] = (0.0, -kappa[15], 0.0)
        row[T_D0] = row[T_D15] = row[T_DR] = 1.0 / 12.0
        row[T_DL] = -1.0 / 12.0
        if p == 0:
            row[T_H0 : T_H0 + 3] = e[0] * np.array((-1.5, 2.0, -0.5))
            row[T_H1 : T_H1 + 4] = e[1] * np.array((-2.0 / 3.0, 1.0 / 48.0, 2.0 / 3.0, -1.0 / 48.0))
            row[T_D0] = row[T_DL] = 0.0
        if p == slabs - 1:
            row[T_H15 : T_H15 + 3] = e[n - 1] * np.array((0.5, -2.0, 1.5))
            row[T_H14 : T_H14 + 4] = e[n - 2] * np.array((1.0 / 48.0, -2.0 / 3.0, -1.0 / 48.0, 2.0 / 3.0))
            row[T_D15] = row[T_DR] = 0.0
    carry = np.zeros((2 * slabs, slabs))
    for p in range(slabs):
        w = 1.0
        for q in range(p - 1, -1, -1):
            carry[p, q] = w
            w *= decay_l[q]
        w = 1.0
        for q in range(p + 1, slabs):
            carry[slabs + p, q] = w
            w *= decay_r[q]
    return table.astype(np.float32), carry.astype(np.float32)


def image_kernel(tiles, base_s, base_v, state, wts, table, xbuf, win, stage):
    tp = tiles + 1
    magic = -(-65536 // tiles)

    def al(x):
        return pl.multiple_of(x, 8)

    for r in range(ROWS):
        xbuf[pl.ds((r * tp + tiles) * 8, 8), :] = jnp.zeros((8, 128), F32)
    for rt in range(2):
        for lt in range(tiles):
            for v in range(VARS):
                xbuf[pl.ds((rt * 8 * tp + lt) * 8 + v, 8, stride=tp * 8), :] = state[
                    v, pl.ds(rt * 8, 8), pl.ds(lt * 128, 128)
                ]

    lane = lax.broadcasted_iota(I32, (8, 128), 1)
    spot = jnp.broadcast_to((base_v[...] & 127).astype(F32), (8, IMAGES)).T
    cols8 = wts[...].T
    for g in range(IMAGES // 8):
        here = spot[g * 8 : g * 8 + 8, 0:1].astype(I32)
        rel = (lane - here) & 127
        w = [jnp.broadcast_to(cols8[g * 8 : g * 8 + 8, k : k + 1], (8, 128)) for k in range(8)]
        for row in range(2):
            m = jnp.zeros((8, 128), F32)
            for k, off in enumerate((0, 1, 96, 97)):
                m = jnp.where(rel == off, w[row * 4 + k], m)
            win[pl.ds(row * IMAGES + g * 8, 8), :] = m

    def image_group(g, _):
        m0 = win[pl.ds(al(g * 8), 8), :]
        m1 = win[pl.ds(al(IMAGES + g * 8), 8), :]
        for k in range(8):
            b = base_s[0, g * 8 + k]
            x = b >> 7
            r = (x * magic) >> 16
            off = al((r * tp + x - r * tiles) * 8)
            inside = lane >= (b & 127)
            z0 = jnp.where(inside, xbuf[pl.ds(off, 8), :], xbuf[pl.ds(al(off + 8), 8), :])
            z1 = jnp.where(
                inside, xbuf[pl.ds(al(off + tp * 8), 8), :], xbuf[pl.ds(al(off + tp * 8 + 8), 8), :]
            )
            stage[pl.ds(al((g * 8 + k) * 8), 8), :] = z0 * m0[k : k + 1, :] + z1 * m1[k : k + 1, :]
        return 0

    lax.fori_loop(0, IMAGES // 8, image_group, 0)

    def half_sum(h, _):
        def node(level, i):
            if level == 0:
                return stage[pl.ds(al((h * 128 + i) * 8), 8), :]
            a = node(level - 1, i)
            b = node(level - 1, i + (128 >> level))
            bit = level - 1
            low = ((lane >> bit) & 1) == 0
            return jnp.where(low, a, b) + pltpu.roll(jnp.where(low, b, a), 128 - (1 << bit), axis=1)

        table[pl.ds(al(h * 8), 8), :] = node(7, 0)
        return 0

    lax.fori_loop(0, 2, half_sum, 0)


def kernel(
    slabs, cross, tiles,
    tab, lam, table, state, phi, cour, mask, gcell, gown, gimg,
    der, seg,
    tabs, req, pick_out, pick_in, gmap, fbuf, xrow, srow, crow, arow,
    coef_out, coef_in, fac, dat_out, dat_in, ret_out, ret_in, halo_out, halo_in,
    send_sem, recv_sem,
):
    p = lax.axis_index("pipe")
    c = lax.axis_index("cross")
    yz, core = p // 2, p % 2
    planes = slabs // 2
    slot = c * 2 + core
    slots = cross * 2
    magic = -(-65536 // tiles)
    groups = tiles // 3
    solvers = -(-(VARS * tiles) // UNITS)
    is_solver = p < solvers

    def send(src, dst, sem, dev):
        pltpu.make_async_remote_copy(
            src_ref=src,
            dst_ref=dst,
            send_sem=send_sem.at[sem],
            recv_sem=recv_sem.at[sem],
            device_id=dev,
            device_id_type=MESH,
        ).start()

    def wait(sems, sem, ref, rows):
        part = ref.at[pl.ds(0, rows), :]
        pltpu.make_async_copy(part, part, sems.at[sem]).wait()

    def al(x):
        return pl.multiple_of(x, 8)

    barrier = pltpu.get_barrier_semaphore()

    def greet(i, _):
        pl.semaphore_signal(barrier, inc=1, device_id=(lax.rem(p + i, slabs), c), device_id_type=MESH)
        return 0

    lax.fori_loop(1, slabs, greet, 0)
    for dc in range(1, cross):
        for k in range(2):
            pl.semaphore_signal(
                barrier, inc=1, device_id=(yz * 2 + k, lax.rem(c + dc, cross)), device_id_type=MESH
            )

    for rt in range(2):
        for lt in range(tiles):
            cols = pl.ds(lt * 128, 128)
            rows = pl.ds(rt * 8, 8)
            solid = mask[rows, cols] == 1
            place = (lt % 3) * 8 + lt // 3
            for v in range(VARS):
                nat = state[v, rows, cols]
                fbuf[pl.ds((v * ROWS + rt * 8) * 24 + place, 8, stride=24), :] = jnp.where(solid, 0.0, nat)
            crow[pl.ds(rt * 8 * 24 + place, 8, stride=24), :] = cour[rows, cols]
            arow[pl.ds(rt * 8 * 24 + place, 8, stride=24), :] = phi[rows, cols]

    tabs[pl.ds(al(slot * 16), 16), :] = table[...]

    req[pl.ds(al(yz * 8), 8), :] = jnp.concatenate(
        [gown[...], gimg[...], jnp.zeros((6, GHOSTS), I32)], axis=0
    )

    pl.semaphore_wait(barrier, slabs - 1 + (cross - 1) * 2)

    for dc in range(cross):
        for dk in range(2):
            if dc or dk:
                send(
                    tabs.at[pl.ds(al(slot * 16), 16), :],
                    tabs.at[pl.ds(al(slot * 16), 16), :],
                    0,
                    (yz * 2 + lax.rem(core + dk, 2), lax.rem(c + dc, cross)),
                )

    def send_req(i, _):
        mine = pl.ds(al(yz * 8), 8)
        send(req.at[mine, :], req.at[mine, :], 1, (lax.rem(yz + i, planes) * 2 + core, c))
        return 0

    lax.fori_loop(1, planes, send_req, 0)

    cell = gcell[...]
    x = cell >> 7
    r = (x * magic) >> 16
    t = x - r * tiles
    t3 = (t * 21846) >> 16
    at_row = r * 24 + (t - t3 * 3) * 8 + t3
    ghost_no = (lax.broadcasted_iota(I32, (1, GHOSTS), 1) + 1).astype(F32)
    row_no = lax.broadcasted_iota(I32, (ROWS * 24, GHOSTS), 0)
    left = jnp.where(row_no == at_row, ghost_no, 0.0).astype(jnp.bfloat16)
    lane_no = lax.broadcasted_iota(I32, (128, GHOSTS), 0)
    right = jnp.where(lane_no == (cell & 127), 1.0, 0.0).astype(jnp.bfloat16)
    numbers = lax.dot_general(left, right, (((1,), (1,)), ((), ())), preferred_element_type=F32)
    gmap[...] = (numbers + 0.5).astype(I32) - 1

    def rowof(ref, i):
        return ref[pl.ds(i * 24, 24), :]

    def put(ref, i, val):
        ref[pl.ds(i * 24, 24), :] = val

    E, H, RD, WL, WR, C = 0, 16, 32, 48, 64, 80
    top = jnp.where(p == slabs - 1, 0.0, 1.0)
    h = rowof(arow, 0)
    m = jnp.ones_like(h)
    m_l = jnp.ones_like(h)
    faces = arow
    for k in range(1, ROWS):
        face = rowof(faces, k)
        if k == ROWS - 1:
            face = face * top
        rd = 1.0 / (h + face + m)
        e = face * rd
        hh = h * rd
        put(arow, 16 + E + k, e)
        put(arow, 16 + H + k, hh)
        put(arow, 16 + RD + k, rd)
        m_l = m_l + m * hh
        h = h * e
        m = 1.0 + m * e
    w_l = jnp.zeros_like(h)
    w_r = jnp.ones_like(h)
    cols = [jnp.zeros_like(h) for _ in range(4)]
    for k in range(ROWS - 1, 0, -1):
        e = rowof(arow, 16 + E + k)
        w_l = rowof(arow, 16 + H + k) + e * w_l
        w_r = e * w_r
        put(arow, 16 + WL + k, w_l)
        put(arow, 16 + WR + k, w_r)
        ck = rowof(crow, k)
        cl, cr = w_l * ck, w_r * ck
        u, v = tab[p, T_U + k], tab[p, T_V + k]
        cols = [cols[0] - u * cl, cols[1] - u * cr, cols[2] - v * cl, cols[3] - v * cr]
        if k == ROWS - 1:
            k1, k2 = -tab[p, T_DR] * cl, -tab[p, T_DR] * cr
    c0 = rowof(crow, 0)
    cols[0] = cols[0] - tab[p, T_U] * c0
    cols[2] = cols[2] - tab[p, T_V] * c0
    fields = [h, m_l, m - 1.0, *cols, -tab[p, T_DL] * c0, k1, k2]
    for k, val in enumerate(fields):
        for b in range(3):
            coef_out[pl.ds(b * 16 + k, 8, stride=48), :] = val[b * 8 : b * 8 + 8, :]

    def first_tile(d):
        return (UNITS * d) // VARS

    def send_coef(i, _):
        d = lax.rem(p + i, slabs)

        @pl.when(d < solvers)
        def _():
            send(
                coef_out.at[pl.ds(al(first_tile(d) * 16), 32), :],
                coef_in.at[pl.ds(al(p * 32), 32), :],
                2,
                (d, c),
            )

        return 0

    lax.fori_loop(1, slabs, send_coef, 0)

    @pl.when(is_solver)
    def _():
        coef_in[pl.ds(al(p * 32), 32), :] = coef_out[pl.ds(al(first_tile(p) * 16), 32), :]

    wait(recv_sem, 0, tabs, (slots - 1) * 16)
    wait(recv_sem, 1, req, (planes - 1) * 8)
    owner = req[pl.ds(0, planes, stride=8), :]
    image = req[pl.ds(1, planes, stride=8), :]
    o_c = lax.rem(owner, cross)
    o_p = lax.div(owner, cross)
    which = jnp.where(
        (o_p >> 1) == yz, (o_c * 2 + (o_p & 1)) * 2 + (image >> 7), jnp.full_like(owner, -1)
    )
    spot7 = jnp.zeros_like(image)
    for bit in range(7):
        spot7 = spot7 | (((image >> bit) & 1) << (6 - bit))
    for n in range(planes):
        idx = jnp.broadcast_to(spot7[n : n + 1, :], (8, 128))
        wh = jnp.broadcast_to(which[n : n + 1, :], (8, 128))
        acc = jnp.zeros((8, 128), F32)
        for k in range(slots * 2):
            got = jnp.take_along_axis(tabs[pl.ds(k * 8, 8), :], idx, axis=1, mode="promise_in_bounds")
            acc = jnp.where(wh == k, got, acc)
        pick_out[pl.ds(n * 8, 8), :] = acc

    def send_pick(i, _):
        n = lax.rem(yz + i, planes)
        send(pick_out.at[pl.ds(al(n * 8), 8), :], pick_in.at[pl.ds(al(yz * 8), 8), :], 3, (n * 2 + core, c))
        return 0

    lax.fori_loop(1, planes, send_pick, 0)
    pick_in[pl.ds(al(yz * 8), 8), :] = pick_out[pl.ds(al(yz * 8), 8), :]

    @pl.when(is_solver)
    def _():
        wait(recv_sem, 2, coef_in, (slabs - 1) * 32)
        for j in range(2):

            def field(k):
                return coef_in[pl.ds(j * 16 + k, slabs, stride=32), :]

            gu = field(0)
            gl = pltpu.roll(gu, 1, axis=0)
            mm = field(1) + pltpu.roll(field(2), 1, axis=0)
            step, s = 0, 1
            while s < slabs:
                rd = 1.0 / (mm + gl + gu)
                pf = gl * pltpu.roll(rd, s, axis=0)
                tf = gu * pltpu.roll(rd, slabs - s, axis=0)
                at0 = ((j * 6 + step) * 2) * slabs
                fac[pl.ds(at0, slabs), :] = pf
                fac[pl.ds(at0 + slabs, slabs), :] = tf
                mm = mm + pf * pltpu.roll(mm, s, axis=0) + tf * pltpu.roll(mm, slabs - s, axis=0)
                gl = pf * pltpu.roll(gl, s, axis=0)
                gu = tf * pltpu.roll(gu, slabs - s, axis=0)
                step, s = step + 1, s * 2
            fac[pl.ds((j * 6 + 5) * 2 * slabs, slabs), :] = 1.0 / (mm + gl + gu)

    wait(recv_sem, 3, pick_in, (planes - 1) * 8)
    ghost = pick_in[pl.ds(0, 8), :]
    for n in range(1, planes):
        ghost = ghost + pick_in[pl.ds(n * 8, 8), :]
    ghost = [jnp.broadcast_to(REFLECT[v] * ghost[v : v + 1, :], (8, 128)) for v in range(VARS)]

    def tv(i):
        return tab[p, i]

    def local(b, _):
        def at(row):
            return pl.ds(al(row * 24 + b * 8), 8)

        def filled(i):
            gi = gmap[at(i), :]
            has = gi >= 0
            idx = jnp.maximum(gi, 0)
            out = []
            for v in range(VARS):
                got = jnp.take_along_axis(ghost[v], idx, axis=1, mode="promise_in_bounds")
                val = jnp.where(has, got, fbuf[at(v * ROWS + i), :])
                fbuf[at(v * ROWS + i), :] = val
                out.append(val)
            return out

        f = [filled(i) for i in range(ROWS)]
        for v in range(VARS):
            fv = [f[i][v] for i in range(ROWS)]
            up = tv(T_K) * fv[0]
            for i in range(ROWS):
                if i == 0:
                    hi = tv(T_H0) * fv[0] + tv(T_H0 + 1) * fv[1] + tv(T_H0 + 2) * fv[2]
                elif i == 1:
                    hi = sum(tv(T_H1 + k) * fv[k] for k in range(4))
                elif i == ROWS - 2:
                    hi = sum(tv(T_H14 + k) * fv[12 + k] for k in range(4))
                elif i == ROWS - 1:
                    hi = sum(tv(T_H15 + k) * fv[13 + k] for k in range(3))
                else:
                    hi = tv(T_K + 1 + i) * (fv[i + 1] - fv[i - 1])
                up = tv(T_R + i) * up + hi
                xrow[at(v * ROWS + i), :] = up
                srow[at(v * ROWS + i), :] = hi
            end = tv(T_K + 1 + ROWS) * fv[ROWS - 1]
            z_l = tv(T_R + ROWS) * up - end
            down = -end
            s_l = s_r = None
            for i in range(ROWS - 1, -1, -1):
                down = tv(T_S + 1 + i) * down
                xi = xrow[at(v * ROWS + i), :] + down
                if i == 0:
                    xi = xi + tv(T_D0) * fv[1]
                elif i == ROWS - 1:
                    xi = xi - tv(T_D15) * fv[ROWS - 2]
                else:
                    xi = xi + (1.0 / 12.0) * (fv[i + 1] - fv[i - 1])
                xrow[at(v * ROWS + i), :] = xi
                down = down + srow[at(v * ROWS + i), :]
                rhs = fv[i] - crow[at(i), :] * xi
                if i:
                    wl, wr = arow[at(16 + WL + i), :], arow[at(16 + WR + i), :]
                    s_l = wl * rhs if s_l is None else s_l + wl * rhs
                    s_r = wr * rhs if s_r is None else s_r + wr * rhs
                else:
                    s_l = s_l + rhs
            z_r = tv(T_S) * down + tv(T_K) * fv[0]
            for k, val in enumerate((z_l, z_r, s_l, s_r, fv[0], fv[ROWS - 1])):
                dat_out[pl.ds((5 * b + v) * 8 + k, 8, stride=120), :] = val
            halo_out[pl.ds(al(v * 24 + b * 8), 8), :] = fv[0]
            halo_out[pl.ds(al(120 + v * 24 + b * 8), 8), :] = fv[ROWS - 1]
        return 0

    lax.fori_loop(0, 3, local, 0)

    def send_dat(i, _):
        d = lax.rem(p + i, slabs)

        @pl.when(d < solvers)
        def _():
            send(
                dat_out.at[pl.ds(al(d * 24), 24), :],
                dat_in.at[pl.ds(al(p * 24), 24), :],
                4,
                (d, c),
            )

        return 0

    lax.fori_loop(1, slabs, send_dat, 0)
    send(halo_out.at[pl.ds(0, 120), :], halo_in.at[pl.ds(0, 120), :], 5, (lax.rem(p + slabs - 1, slabs), c))
    send(halo_out.at[pl.ds(120, 120), :], halo_in.at[pl.ds(120, 120), :], 6, (lax.rem(p + 1, slabs), c))

    @pl.when(is_solver)
    def _():
        dat_in[pl.ds(al(p * 24), 24), :] = dat_out[pl.ds(al(p * 24), 24), :]
        wait(recv_sem, 4, dat_in, (slabs - 1) * 24)

        def data(u, k):
            return dat_in[pl.ds(u * 8 + k, slabs, stride=24), :]

        z_l = jnp.concatenate([data(u, 0) for u in range(UNITS)], axis=1)
        z_r = jnp.concatenate([data(u, 1) for u in range(UNITS)], axis=1)
        hi = lax.Precision.HIGHEST
        c_l = jnp.dot(lam[pl.ds(0, slabs), :], z_l, precision=hi, preferred_element_type=F32)
        c_r = jnp.dot(lam[pl.ds(slabs, slabs), :], z_r, precision=hi, preferred_element_type=F32)
        for u in range(UNITS):
            j = (UNITS * p + u) // VARS - first_tile(p)

            def field(k):
                return coef_in[pl.ds(j * 16 + k, slabs, stride=32), :]

            cl, cr = c_l[:, u * 128 : u * 128 + 128], c_r[:, u * 128 : u * 128 + 128]
            f_up = pltpu.roll(data(u, 4), slabs - 1, axis=0)
            f_dn = pltpu.roll(data(u, 5), 1, axis=0)
            q = data(u, 3) + field(4) * cl + field(6) * cr + field(9) * f_up
            d = data(u, 2) + field(3) * cl + field(5) * cr + field(7) * f_dn + field(8) * f_up
            d = d + pltpu.roll(q, 1, axis=0)
            step, s = 0, 1
            while s < slabs:
                at0 = ((j * 6 + step) * 2) * slabs
                pf = fac[pl.ds(al(at0), slabs), :]
                tf = fac[pl.ds(al(at0 + slabs), slabs), :]
                d = d + pf * pltpu.roll(d, s, axis=0) + tf * pltpu.roll(d, slabs - s, axis=0)
                step, s = step + 1, s * 2
            x = d * fac[pl.ds(al((j * 6 + 5) * 2 * slabs), slabs), :]
            for k, val in enumerate((cl, cr, x, pltpu.roll(x, slabs - 1, axis=0))):
                ret_out[pl.ds(u * 4 + k, slabs, stride=16), :] = val

        def send_ret(i, _):
            d = lax.rem(p + i, slabs)
            send(ret_out.at[pl.ds(al(d * 16), 16), :], ret_in.at[pl.ds(al(p * 16), 16), :], 7, (d, c))
            return 0

        lax.fori_loop(1, slabs, send_ret, 0)
        ret_in[pl.ds(al(p * 16), 16), :] = ret_out[pl.ds(al(p * 16), 16), :]
        wait(recv_sem, 7, ret_in, (solvers - 1) * 16)

    @pl.when(jnp.logical_not(is_solver))
    def _():
        wait(recv_sem, 7, ret_in, solvers * 16)

    wait(recv_sem, 5, halo_in, 120)
    wait(recv_sem, 6, halo_in, 120)

    def finish(b, _):
        def at(row):
            return pl.ds(al(row * 24 + b * 8), 8)

        for v in range(VARS):
            w = 5 * b + v

            def back(k):
                return ret_in[pl.ds((w // 3) * 16 + (w % 3) * 4 + k, 8, stride=80), :]

            left_c, right_c, t0, t1 = back(0), back(1), back(2), back(3)
            above = halo_in[at(v), :]
            below = halo_in[at(5 + v), :]
            run = None
            for i in range(ROWS):
                xi = xrow[at(v * ROWS + i), :] + tv(T_U + i) * left_c + tv(T_V + i) * right_c
                if i == 0:
                    xi = xi + tv(T_DL) * below
                if i == ROWS - 1:
                    xi = xi + tv(T_DR) * above
                xrow[at(v * ROWS + i), :] = xi
                if i:
                    rhs = fbuf[at(v * ROWS + i), :] - crow[at(i), :] * xi
                    run = rhs if run is None else rhs + arow[at(16 + E + i - 1), :] * run
                    srow[at(v * ROWS + i), :] = (
                        arow[at(16 + RD + i), :] * run + arow[at(16 + H + i), :] * t0
                    )
            y = t1
            for i in range(ROWS - 1, 0, -1):
                y = srow[at(v * ROWS + i), :] + arow[at(16 + E + i), :] * y
                srow[at(v * ROWS + i), :] = y
            srow[at(v * ROWS), :] = t0
        return 0

    lax.fori_loop(0, 3, finish, 0)
    for v in range(VARS):
        for rt in range(2):
            for lt in range(tiles):
                src = pl.ds((v * ROWS + rt * 8) * 24 + (lt % 3) * 8 + lt // 3, 8, stride=24)
                der[v, pl.ds(rt * 8, 8), pl.ds(lt * 128, 128)] = xrow[src, :]
                seg[v, pl.ds(rt * 8, 8), pl.ds(lt * 128, 128)] = srow[src, :]

    wait(send_sem, 0, tabs, (slots - 1) * 16)
    wait(send_sem, 1, req, (planes - 1) * 8)
    wait(send_sem, 3, pick_in, (planes - 1) * 8)
    wait(send_sem, 5, halo_in, 120)
    wait(send_sem, 6, halo_in, 120)

    @pl.when(is_solver)
    def _():
        wait(send_sem, 2, coef_in, (solvers - 1) * 32)
        wait(send_sem, 4, dat_in, (solvers - 1) * 24)
        wait(send_sem, 7, ret_out, (slabs - 1) * 16)

    @pl.when(jnp.logical_not(is_solver))
    def _():
        wait(send_sem, 2, coef_in, solvers * 32)
        wait(send_sem, 4, dat_in, solvers * 24)


def solution(mesh):
    slabs, cross = mesh.shape["pipe"], mesh.shape["cross"]
    table, carry = derivative_constants(slabs)

    def local(state, face, courant, cell_mask, ghost_cell, ghost_owner, ghost_image, base, weight):
        pencils = state.shape[2]
        tiles = pencils // 128
        solvers = -(-(VARS * tiles) // UNITS)
        vm = pl.BlockSpec(memory_space=pltpu.VMEM)
        sm = pl.BlockSpec(memory_space=pltpu.SMEM)
        out = jax.ShapeDtypeStruct(state.shape, F32)
        planes, slots = slabs // 2, cross * 2
        span = VARS * ROWS * 24

        def buf(rows, dtype=F32):
            return pltpu.VMEM((rows, 128), dtype)

        base = base.reshape(1, -1)
        images = pl.pallas_call(
            functools.partial(image_kernel, tiles),
            out_shape=jax.ShapeDtypeStruct((16, 128), F32),
            in_specs=[sm, vm, vm, vm],
            out_specs=vm,
            scratch_shapes=[
                buf(ROWS * (tiles + 1) * 8),
                buf(2 * IMAGES),
                buf(IMAGES * 8),
            ],
            compiler_params=pltpu.CompilerParams(vmem_limit_bytes=24 * 1024 * 1024),
        )(base, base, state, weight)
        return pl.pallas_call(
            functools.partial(kernel, slabs, cross, tiles),
            out_shape=(out, out),
            in_specs=[sm] + [vm] * 9,
            out_specs=(vm, vm),
            scratch_shapes=[
                buf(slots * 16),
                buf(planes * 8, I32),
                buf(planes * 8),
                buf(planes * 8),
                buf(ROWS * 24, I32),
                buf(span),
                buf(span),
                buf(span),
                buf(ROWS * 24),
                buf(ROWS * 24 * 6),
                buf(384),
                buf(slabs * 32),
                buf(24 * slabs),
                buf(960),
                buf(slabs * 24),
                buf(slabs * 16),
                buf(max(640, solvers * 16)),
                buf(240),
                buf(240),
                pltpu.SemaphoreType.DMA((8,)),
                pltpu.SemaphoreType.DMA((8,)),
            ],
            compiler_params=pltpu.CompilerParams(
                collective_id=0, has_side_effects=True, vmem_limit_bytes=40 * 1024 * 1024
            ),
        )(
            jnp.asarray(table), jnp.asarray(carry), images,
            state, face, courant, cell_mask,
            ghost_cell.reshape(1, -1), ghost_owner.reshape(1, -1), ghost_image.reshape(1, -1),
        )

    flat = P(("pipe", "cross"))
    slab = P("pipe", "cross")
    whole = P(None, "pipe", "cross")
    return jax.shard_map(
        local,
        mesh=mesh,
        in_specs=(whole, slab, slab, slab, flat, flat, flat, flat, P(None, ("pipe", "cross"))),
        out_specs=(whole, whole),
        check_vma=False,
    )
```

time: 694 us -> 49.5 us (0.07)
  waiting for transfers between devices: 383 us -> 0 us
  starting transfers between devices: 113 us -> 0 us
  blocking collectives: 108 us -> 0 us
  other arithmetic: 49 us -> 0 us
  Pallas kernels: 0 us -> 40.7 us
  local copies, waits for them, and re-layouts: 36.3 us -> 7.71 us
    ppermute x38 -> x0, waiting for transfers between devices: 383 us -> none  [the longest x20 329 us: passed_along(): return lax.ppermute(block, axis, route)]
    ppermute x38 -> x0, starting transfers between devices: 113 us -> none  [the longest x20 68.8 us: passed_along(): return lax.ppermute(block, axis, route)]
    all_gather x1 -> x0, blocking collectives: 108 us -> none  [local(): lax.all_gather(image_values, ('pipe', 'cross'), axis=1, tiled=True)]
    pallas_call x0 -> x2, Pallas kernels: none -> 40.7 us  [the longest x1 37.4 us: local(): pl.pallas_call(functools.partial(kernel, slabs, cross, tiles), out_shape=...]
    select_n x4 -> x0, other arithmetic: 21.1 us -> none  [the longest x1 21.1 us: local(): cleared = jnp.where(cell_mask.reshape(1, -1) == 1, 0.0, flat_state)]
    scatter x1 -> x0, other arithmetic: 14.8 us -> none  [local(): cleared.at[:, ghost_cell].set(reflection * picked)]
    gather x1 -> x0, local copies, waits for them, and re-layouts: 11.8 us -> none  [local(): image_values = jnp.sum(flat_state[:, corners] * image_weight[None], axis=1)]
    reshape x1 -> x0, local copies, waits for them, and re-layouts: 11.1 us -> none  [local(): cleared.at[:, ghost_cell].set(reflection * picked)]
  transfers between devices with their start and end apart: 38 -> 0, of which waited for: 31 -> 0; matrix products, arithmetic and copies ran while one was open for 1% -> 0% of each run, Pallas kernels for 0% -> 0%
where the time goes in v1:
time: 49.5 us; the launch traced here: 49.2 us
  Pallas kernels  40.7 us (82%)
  local copies, waits for them, and re-layouts  7.71 us (16%)
  between operations  0.7 us (1%)
    pallas_call x1, Pallas kernels, local(): pl.pallas_call(functools.partial(kernel, slabs, cross, tiles), out_shape=...  37.4 us
    unnamed x26, local copies, waits for them, and re-layouts  7.71 us
    pallas_call x1, Pallas kernels, local(): pl.pallas_call(functools.partial(image_kernel, tiles), out_shape=jax.Shap...  3.38 us

profile of v1, /device:TPU:1, one launch (start us, length us, event | category | flops | bytes accessed | tf_op | source)
XLA Modules:
  0.0 49.2 jit_solution(451815613821010651)
XLA Ops:
  0.6 0.0 copy-start.8
  0.6 0.7 %copy-done.8 = s32[256]{0:T(256)S(1)} copy-done((s32[256]{0:T(256)S(1)}, s32[256]{0:T(256)}, u32[]{:S(2)}) %copy-start.8) | copy-done | bytes 1048
  1.3 0.0 copy-start
  1.3 1.1 %copy-done = f32[5,16,2304]{2,1,0:T(8,128)S(1)} copy-done((f32[5,16,2304]{2,1,0:T(8,128)S(1)}, f32[5,16,2304]{2,1,0:T(8,128)}, u32[]{:S(2)}) %copy-start) | copy-done | bytes 737304
  2.4 0.0 copy-start.7
  2.4 0.7 %copy-done.7 = f32[8,256]{1,0:T(8,128)S(1)} copy-done((f32[8,256]{1,0:T(8,128)S(1)}, f32[8,256]{1,0:T(8,128)}, u32[]{:S(2)}) %copy-start.7) | copy-done | bytes 8216
  3.1 0.0 copy-start.1
  3.1 0.0 copy-start.6
  3.1 0.0 copy-start.9
  3.1 0.0 copy-start.10
  3.1 0.0 copy-start.11
  3.1 3.4 %shard_map.122.table = f32[16,128]{1,0:T(8,128)S(1)} custom-call(s32[1,256]{1,0:T(1,128)S(1)} %bitcast.4, s32[1,256]{1,0:T(1,128)S(1)} %bitcast.5, f32[5,16,2304]{2,1,0:T(8,128)S(1)} %copy-done, f32[8,256]{1,0:T(8,128)S(1)} %copy-done.7), custom_call_target="tpu_custom_call" | custom-call | tf_op jit(solution)/shard_map/pallas_call | solution.py:606
  6.5 0.0 copy-done.1
  6.5 0.0 copy-done.6
  6.5 0.0 copy-done.9
  6.5 0.0 copy-done.10
  6.6 0.0 copy-done.11
  6.6 0.0 copy-start.2
  6.6 0.9 %copy-done.2 = f32[16,2304]{1,0:T(8,128)S(1)} copy-done((f32[16,2304]{1,0:T(8,128)S(1)}, f32[16,2304]{1,0:T(8,128)}, u32[]{:S(2)}) %copy-start.2) | copy-done | bytes 147480
  7.5 0.0 copy-start.3
  7.5 0.9 %copy-done.3 = f32[16,2304]{1,0:T(8,128)S(1)} copy-done((f32[16,2304]{1,0:T(8,128)S(1)}, f32[16,2304]{1,0:T(8,128)}, u32[]{:S(2)}) %copy-start.3) | copy-done | bytes 147480
  8.4 0.0 copy-start.4
  8.4 0.9 %copy-done.4 = s32[16,2304]{1,0:T(8,128)S(1)} copy-done((s32[16,2304]{1,0:T(8,128)S(1)}, s32[16,2304]{1,0:T(8,128)}, u32[]{:S(2)}) %copy-start.4) | copy-done | bytes 147480
  9.3 0.0 copy-start.5
  9.3 0.8 %copy-done.5 = f32[64,32]{1,0:T(8,128)S(1)} copy-done((f32[64,32]{1,0:T(8,128)S(1)}, f32[64,32]{1,0:T(8,128)}, u32[]{:S(2)}) %copy-start.5) | copy-done | bytes 8216
  10.1 37.4 %shard_map.123 = (f32[5,16,2304]{2,1,0:T(8,128)S(1)}, f32[5,16,2304]{2,1,0:T(8,128)S(1)}) custom-call(f32[32,128]{1,0:T(8,128)S(1)} %copy-done.6, f32[64,32]{1,0:T(8,128)S(1)} %copy-done.5, f32[16,128]{1,0:T(8,128)S(1)} %shard_map.122.table, f32[5,16,2304]{2,1,0:T(8,128)S(1)} %copy-done.1, f32[16,2304]{1,0:T(8,128)S(1)} %copy-done.2, ...), custom_call_target="tpu_custom_call" | custom-call | tf_op jit(solution)/shard_map/pallas_call | solution.py:618
  47.4 0.9 %copy.15 = f32[5,16,2304]{2,1,0:T(8,128)} copy(f32[5,16,2304]{2,1,0:T(8,128)S(1)} %get-tuple-element.4) | data formatting | bytes 1474560
  48.3 0.9 %copy.16 = f32[5,16,2304]{2,1,0:T(8,128)} copy(f32[5,16,2304]{2,1,0:T(8,128)S(1)} %get-tuple-element.5) | data formatting | bytes 1474560
Async XLA Ops:
  0.6 0.7 %copy-start.8 = (s32[256]{0:T(256)S(1)}, s32[256]{0:T(256)}, u32[]{:S(2)}) copy-start(s32[256]{0:T(256)} %param.18) | copy-start | bytes 3076
  1.3 1.1 %copy-start = (f32[5,16,2304]{2,1,0:T(8,128)S(1)}, f32[5,16,2304]{2,1,0:T(8,128)}, u32[]{:S(2)}) copy-start(f32[5,16,2304]{2,1,0:T(8,128)} %state.3) | copy-start | bytes 2211844
  2.4 0.7 %copy-start.7 = (f32[8,256]{1,0:T(8,128)S(1)}, f32[8,256]{1,0:T(8,128)}, u32[]{:S(2)}) copy-start(f32[8,256]{1,0:T(8,128)} %wts.1) | copy-start | bytes 24580
  3.1 3.4 %copy-start.1 = (f32[5,16,2304]{2,1,0:T(8,128)S(1)}, f32[5,16,2304]{2,1,0:T(8,128)}, u32[]{:S(2)}) copy-start(f32[5,16,2304]{2,1,0:T(8,128)} %state.3) | copy-start | bytes 2211844
  3.1 3.4 %copy-start.6 = (f32[32,128]{1,0:T(8,128)S(1)}, f32[32,128]{1,0:T(8,128)}, u32[]{:S(2)}) copy-start(f32[32,128]{1,0:T(8,128)} %constant.4.clone.tab) | copy-start | bytes 49156
  3.1 3.4 %copy-start.9 = (s32[128]{0:T(128)S(1)}, s32[128]{0:T(128)}, u32[]{:S(2)}) copy-start(s32[128]{0:T(128)} %param.15) | copy-start | bytes 1540
  3.1 3.4 %copy-start.10 = (s32[128]{0:T(128)S(1)}, s32[128]{0:T(128)}, u32[]{:S(2)}) copy-start(s32[128]{0:T(128)} %param.16) | copy-start | bytes 1540
  3.1 3.4 %copy-start.11 = (s32[128]{0:T(128)S(1)}, s32[128]{0:T(128)}, u32[]{:S(2)}) copy-start(s32[128]{0:T(128)} %param.17) | copy-start | bytes 1540
  6.6 0.9 %copy-start.2 = (f32[16,2304]{1,0:T(8,128)S(1)}, f32[16,2304]{1,0:T(8,128)}, u32[]{:S(2)}) copy-start(f32[16,2304]{1,0:T(8,128)} %phi.1) | copy-start | bytes 442372
  7.5 0.9 %copy-start.3 = (f32[16,2304]{1,0:T(8,128)S(1)}, f32[16,2304]{1,0:T(8,128)}, u32[]{:S(2)}) copy-start(f32[16,2304]{1,0:T(8,128)} %cour.1) | copy-start | bytes 442372
  8.4 0.9 %copy-start.4 = (s32[16,2304]{1,0:T(8,128)S(1)}, s32[16,2304]{1,0:T(8,128)}, u32[]{:S(2)}) copy-start(s32[16,2304]{1,0:T(8,128)} %mask.1) | copy-start | bytes 442372
  9.3 0.8 %copy-start.5 = (f32[64,32]{1,0:T(8,128)S(1)}, f32[64,32]{1,0:T(8,128)}, u32[]{:S(2)}) copy-start(f32[64,32]{1,0:T(8,128)} %constant.5.clone.lam) | copy-start | bytes 24580

commit v2 on v1

--- a/solution.py
+++ b/solution.py
@@ -93,23 +93,80 @@
     return table.astype(np.float32), carry.astype(np.float32)
 
 
-def image_kernel(tiles, base_s, base_v, state, wts, table, xbuf, win, stage):
+def kernel(
+    slabs, cross, tiles,
+    tab_hbm, lam_hbm, base_hbm, state_hbm, phi_hbm, cour_hbm, mask_hbm, gcell_hbm, gown_hbm, gimg_hbm, wts_hbm,
+    der, seg,
+    tab, base_s, lam, base_v, state, phi, cour, mask, gcell, gown, gimg, wts,
+    xbuf, win, stage, tabs, req, pick_out, pick_in, gmap, fbuf, xrow, srow, crow, arow,
+    coef_out, coef_in, fac, side_out, side_in, dat_out, dat_in, ret_out, ret_in, halo_out, halo_in,
+    in_sem, send_sem, recv_sem,
+):
+    p = lax.axis_index("pipe")
+    c = lax.axis_index("cross")
+    yz, core = p // 2, p % 2
+    planes = slabs // 2
+    slot = c * 2 + core
+    slots = cross * 2
     tp = tiles + 1
     magic = -(-65536 // tiles)
+    solvers = -(-(VARS * tiles) // UNITS)
+    is_solver = p < solvers
+    before, after = lax.rem(p + slabs - 1, slabs), lax.rem(p + 1, slabs)
+
+    def fetch(k, src, dst):
+        copy = pltpu.make_async_copy(src, dst, in_sem.at[k])
+        copy.start()
+        return copy
+
+    got_state = fetch(0, state_hbm, state)
+    got_base = fetch(1, base_hbm, base_v)
+    got_base_s = fetch(2, base_hbm, base_s)
+    got_wts = fetch(3, wts_hbm, wts)
+    got_rest = [
+        fetch(4, mask_hbm, mask),
+        fetch(5, phi_hbm, phi),
+        fetch(6, cour_hbm, cour),
+        fetch(7, gcell_hbm, gcell),
+        fetch(8, gown_hbm, gown),
+        fetch(9, gimg_hbm, gimg),
+        fetch(10, tab_hbm.at[p], tab),
+        fetch(11, lam_hbm, lam),
+    ]
+
+    def send(src, dst, sem, dev):
+        pltpu.make_async_remote_copy(
+            src_ref=src,
+            dst_ref=dst,
+            send_sem=send_sem.at[sem],
+            recv_sem=recv_sem.at[sem],
+            device_id=dev,
+            device_id_type=MESH,
+        ).start()
+
+    def wait(sems, sem, ref, rows):
+        part = ref.at[pl.ds(0, rows), :]
+        pltpu.make_async_copy(part, part, sems.at[sem]).wait()
 
     def al(x):
         return pl.multiple_of(x, 8)
 
-    for r in range(ROWS):
-        xbuf[pl.ds((r * tp + tiles) * 8, 8), :] = jnp.zeros((8, 128), F32)
-    for rt in range(2):
-        for lt in range(tiles):
-            for v in range(VARS):
-                xbuf[pl.ds((rt * 8 * tp + lt) * 8 + v, 8, stride=tp * 8), :] = state[
-                    v, pl.ds(rt * 8, 8), pl.ds(lt * 128, 128)
-                ]
+    barrier = pltpu.get_barrier_semaphore()
+
+    def greet(i, _):
+        pl.semaphore_signal(barrier, inc=1, device_id=(lax.rem(p + i, slabs), c), device_id_type=MESH)
+        return 0
+
+    lax.fori_loop(1, slabs, greet, 0)
+    for dc in range(1, cross):
+        for k in range(2):
+            pl.semaphore_signal(
+                barrier, inc=1, device_id=(yz * 2 + k, lax.rem(c + dc, cross)), device_id_type=MESH
+            )
 
     lane = lax.broadcasted_iota(I32, (8, 128), 1)
+    got_base.wait()
+    got_wts.wait()
     spot = jnp.broadcast_to((base_v[...] & 127).astype(F32), (8, IMAGES)).T
     cols8 = wts[...].T
     for g in range(IMAGES // 8):
@@ -122,6 +179,17 @@
                 m = jnp.where(rel == off, w[row * 4 + k], m)
             win[pl.ds(row * IMAGES + g * 8, 8), :] = m
 
+    for r in range(ROWS):
+        xbuf[pl.ds((r * tp + tiles) * 8, 8), :] = jnp.zeros((8, 128), F32)
+    got_state.wait()
+    for rt in range(2):
+        for lt in range(tiles):
+            for v in range(VARS):
+                nat = state[v, pl.ds(rt * 8, 8), pl.ds(lt * 128, 128)]
+                xbuf[pl.ds((rt * 8 * tp + lt) * 8 + v, 8, stride=tp * 8), :] = nat
+    got_base_s.wait()
+    blocks = xbuf.reshape(ROWS * tp, 8, 128)
+
     def image_group(g, _):
         m0 = win[pl.ds(al(g * 8), 8), :]
         m1 = win[pl.ds(al(IMAGES + g * 8), 8), :]
@@ -129,12 +197,10 @@
             b = base_s[0, g * 8 + k]
             x = b >> 7
             r = (x * magic) >> 16
-            off = al((r * tp + x - r * tiles) * 8)
+            off = x + r
             inside = lane >= (b & 127)
-            z0 = jnp.where(inside, xbuf[pl.ds(off, 8), :], xbuf[pl.ds(al(off + 8), 8), :])
-            z1 = jnp.where(
-                inside, xbuf[pl.ds(al(off + tp * 8), 8), :], xbuf[pl.ds(al(off + tp * 8 + 8), 8), :]
-            )
+            z0 = jnp.where(inside, blocks[off], blocks[off + 1])
+            z1 = jnp.where(inside, blocks[off + tp], blocks[off + tp + 1])
             stage[pl.ds(al((g * 8 + k) * 8), 8), :] = z0 * m0[k : k + 1, :] + z1 * m1[k : k + 1, :]
         return 0
 
@@ -150,75 +216,13 @@
             low = ((lane >> bit) & 1) == 0
             return jnp.where(low, a, b) + pltpu.roll(jnp.where(low, b, a), 128 - (1 << bit), axis=1)
 
-        table[pl.ds(al(h * 8), 8), :] = node(7, 0)
+        tabs[pl.ds(al((slot * 2 + h) * 8), 8), :] = node(7, 0)
         return 0
 
     lax.fori_loop(0, 2, half_sum, 0)
 
-
-def kernel(
-    slabs, cross, tiles,
-    tab, lam, table, state, phi, cour, mask, gcell, gown, gimg,
-    der, seg,
-    tabs, req, pick_out, pick_in, gmap, fbuf, xrow, srow, crow, arow,
-    coef_out, coef_in, fac, dat_out, dat_in, ret_out, ret_in, halo_out, halo_in,
-    send_sem, recv_sem,
-):
-    p = lax.axis_index("pipe")
-    c = lax.axis_index("cross")
-    yz, core = p // 2, p % 2
-    planes = slabs // 2
-    slot = c * 2 + core
-    slots = cross * 2
-    magic = -(-65536 // tiles)
-    groups = tiles // 3
-    solvers = -(-(VARS * tiles) // UNITS)
-    is_solver = p < solvers
-
-    def send(src, dst, sem, dev):
-        pltpu.make_async_remote_copy(
-            src_ref=src,
-            dst_ref=dst,
-            send_sem=send_sem.at[sem],
-            recv_sem=recv_sem.at[sem],
-            device_id=dev,
-            device_id_type=MESH,
-        ).start()
-
-    def wait(sems, sem, ref, rows):
-        part = ref.at[pl.ds(0, rows), :]
-        pltpu.make_async_copy(part, part, sems.at[sem]).wait()
-
-    def al(x):
-        return pl.multiple_of(x, 8)
-
-    barrier = pltpu.get_barrier_semaphore()
-
-    def greet(i, _):
-        pl.semaphore_signal(barrier, inc=1, device_id=(lax.rem(p + i, slabs), c), device_id_type=MESH)
-        return 0
-
-    lax.fori_loop(1, slabs, greet, 0)
-    for dc in range(1, cross):
-        for k in range(2):
-            pl.semaphore_signal(
-                barrier, inc=1, device_id=(yz * 2 + k, lax.rem(c + dc, cross)), device_id_type=MESH
-            )
-
-    for rt in range(2):
-        for lt in range(tiles):
-            cols = pl.ds(lt * 128, 128)
-            rows = pl.ds(rt * 8, 8)
-            solid = mask[rows, cols] == 1
-            place = (lt % 3) * 8 + lt // 3
-            for v in range(VARS):
-                nat = state[v, rows, cols]
-                fbuf[pl.ds((v * ROWS + rt * 8) * 24 + place, 8, stride=24), :] = jnp.where(solid, 0.0, nat)
-            crow[pl.ds(rt * 8 * 24 + place, 8, stride=24), :] = cour[rows, cols]
-            arow[pl.ds(rt * 8 * 24 + place, 8, stride=24), :] = phi[rows, cols]
-
-    tabs[pl.ds(al(slot * 16), 16), :] = table[...]
-
+    for copy in got_rest:
+        copy.wait()
     req[pl.ds(al(yz * 8), 8), :] = jnp.concatenate(
         [gown[...], gimg[...], jnp.zeros((6, GHOSTS), I32)], axis=0
     )
@@ -241,6 +245,19 @@
         return 0
 
     lax.fori_loop(1, planes, send_req, 0)
+
+    for rt in range(2):
+        for lt in range(tiles):
+            cols = pl.ds(lt * 128, 128)
+            rows = pl.ds(rt * 8, 8)
+            solid = mask[rows, cols] == 1
+            place = (lt % 3) * 8 + lt // 3
+            for v in range(VARS):
+                fbuf[pl.ds((v * ROWS + rt * 8) * 24 + place, 8, stride=24), :] = jnp.where(
+                    solid, 0.0, state[v, rows, cols]
+                )
+            crow[pl.ds(rt * 8 * 24 + place, 8, stride=24), :] = cour[rows, cols]
+            arow[pl.ds(rt * 8 * 24 + place, 8, stride=24), :] = phi[rows, cols]
 
     cell = gcell[...]
     x = cell >> 7
@@ -292,40 +309,26 @@
         put(arow, 16 + WR + k, w_r)
         ck = rowof(crow, k)
         cl, cr = w_l * ck, w_r * ck
-        u, v = tab[p, T_U + k], tab[p, T_V + k]
+        u, v = tab[0, T_U + k], tab[0, T_V + k]
         cols = [cols[0] - u * cl, cols[1] - u * cr, cols[2] - v * cl, cols[3] - v * cr]
         if k == ROWS - 1:
-            k1, k2 = -tab[p, T_DR] * cl, -tab[p, T_DR] * cr
+            k1, k2 = -tab[0, T_DR] * cl, -tab[0, T_DR] * cr
     c0 = rowof(crow, 0)
-    cols[0] = cols[0] - tab[p, T_U] * c0
-    cols[2] = cols[2] - tab[p, T_V] * c0
-    fields = [h, m_l, m - 1.0, *cols, -tab[p, T_DL] * c0, k1, k2]
-    for k, val in enumerate(fields):
+    cols[0] = cols[0] - tab[0, T_U] * c0
+    cols[2] = cols[2] - tab[0, T_V] * c0
+    for k, val in enumerate((h, m_l, m - 1.0, *cols)):
         for b in range(3):
-            coef_out[pl.ds(b * 16 + k, 8, stride=48), :] = val[b * 8 : b * 8 + 8, :]
+            coef_out[pl.ds(b * 8 + k, 8, stride=24), :] = val[b * 8 : b * 8 + 8, :]
+    for k, val in enumerate((-tab[0, T_DL] * c0, k1, k2)):
+        side_out[pl.ds(k * 24, 24), :] = val
 
     def first_tile(d):
         return (UNITS * d) // VARS
 
-    def send_coef(i, _):
-        d = lax.rem(p + i, slabs)
-
-        @pl.when(d < solvers)
-        def _():
-            send(
-                coef_out.at[pl.ds(al(first_tile(d) * 16), 32), :],
-                coef_in.at[pl.ds(al(p * 32), 32), :],
-                2,
-                (d, c),
-            )
-
-        return 0
-
-    lax.fori_loop(1, slabs, send_coef, 0)
-
-    @pl.when(is_solver)
-    def _():
-        coef_in[pl.ds(al(p * 32), 32), :] = coef_out[pl.ds(al(first_tile(p) * 16), 32), :]
+    def has_two(d):
+        return jnp.logical_and(d < solvers, lax.rem(UNITS * d, VARS) > VARS - UNITS)
+
+    n_two = sum((UNITS * d) % VARS > VARS - UNITS for d in range(solvers))
 
     wait(recv_sem, 0, tabs, (slots - 1) * 16)
     wait(recv_sem, 1, req, (planes - 1) * 8)
@@ -356,30 +359,36 @@
     lax.fori_loop(1, planes, send_pick, 0)
     pick_in[pl.ds(al(yz * 8), 8), :] = pick_out[pl.ds(al(yz * 8), 8), :]
 
+    def send_coef(i, _):
+        d = lax.rem(p + i, slabs)
+
+        @pl.when(d < solvers)
+        def _():
+            send(
+                coef_out.at[pl.ds(al(first_tile(d) * 8), 8), :],
+                coef_in.at[pl.ds(al(p * 16), 8), :],
+                2,
+                (d, c),
+            )
+
+        @pl.when(has_two(d))
+        def _():
+            send(
+                coef_out.at[pl.ds(al(first_tile(d) * 8 + 8), 8), :],
+                coef_in.at[pl.ds(al(p * 16 + 8), 8), :],
+                8,
+                (d, c),
+            )
+
+        return 0
+
+    send(side_out.at[pl.ds(0, 24), :], side_in.at[pl.ds(0, 24), :], 9, (before, c))
+    send(side_out.at[pl.ds(24, 48), :], side_in.at[pl.ds(24, 48), :], 10, (after, c))
+    lax.fori_loop(1, slabs, send_coef, 0)
+
     @pl.when(is_solver)
     def _():
-        wait(recv_sem, 2, coef_in, (slabs - 1) * 32)
-        for j in range(2):
-
-            def field(k):
-                return coef_in[pl.ds(j * 16 + k, slabs, stride=32), :]
-
-            gu = field(0)
-            gl = pltpu.roll(gu, 1, axis=0)
-            mm = field(1) + pltpu.roll(field(2), 1, axis=0)
-            step, s = 0, 1
-            while s < slabs:
-                rd = 1.0 / (mm + gl + gu)
-                pf = gl * pltpu.roll(rd, s, axis=0)
-                tf = gu * pltpu.roll(rd, slabs - s, axis=0)
-                at0 = ((j * 6 + step) * 2) * slabs
-                fac[pl.ds(at0, slabs), :] = pf
-                fac[pl.ds(at0 + slabs, slabs), :] = tf
-                mm = mm + pf * pltpu.roll(mm, s, axis=0) + tf * pltpu.roll(mm, slabs - s, axis=0)
-                gl = pf * pltpu.roll(gl, s, axis=0)
-                gu = tf * pltpu.roll(gu, slabs - s, axis=0)
-                step, s = step + 1, s * 2
-            fac[pl.ds((j * 6 + 5) * 2 * slabs, slabs), :] = 1.0 / (mm + gl + gu)
+        coef_in[pl.ds(al(p * 16), 16), :] = coef_out[pl.ds(al(first_tile(p) * 8), 16), :]
 
     wait(recv_sem, 3, pick_in, (planes - 1) * 8)
     ghost = pick_in[pl.ds(0, 8), :]
@@ -388,7 +397,27 @@
     ghost = [jnp.broadcast_to(REFLECT[v] * ghost[v : v + 1, :], (8, 128)) for v in range(VARS)]
 
     def tv(i):
-        return tab[p, i]
+        return tab[0, i]
+
+    wait(recv_sem, 9, side_in, 24)
+    wait(recv_sem, 10, side_in, 48)
+
+    def send_class(k):
+        def one(i, _):
+            d = 5 * lax.rem(p + i, tiles // 3) + k
+
+            @pl.when(d != p)
+            def _():
+                send(
+                    dat_out.at[pl.ds(al(d * 16), 16), :],
+                    dat_in.at[pl.ds(al(p * 16), 16), :],
+                    4,
+                    (d, c),
+                )
+
+            return 0
+
+        lax.fori_loop(0, tiles // 3, one, 0)
 
     def local(b, _):
         def at(row):
@@ -447,39 +476,64 @@
                 else:
                     s_l = s_l + rhs
             z_r = tv(T_S) * down + tv(T_K) * fv[0]
-            for k, val in enumerate((z_l, z_r, s_l, s_r, fv[0], fv[ROWS - 1])):
-                dat_out[pl.ds((5 * b + v) * 8 + k, 8, stride=120), :] = val
+            s_r = s_r + side_in[at(0), :] * fv[ROWS - 1]
+            s_b = side_in[at(1), :] * fv[0]
+            s_l = s_l + side_in[at(2), :] * fv[0]
+            w = 5 * b + v
+            for k, val in enumerate((z_l, z_r, s_l, s_r, s_b)):
+                dat_out[pl.ds((w // 3) * 16 + (w % 3) * 5 + k, 8, stride=80), :] = val
             halo_out[pl.ds(al(v * 24 + b * 8), 8), :] = fv[0]
             halo_out[pl.ds(al(120 + v * 24 + b * 8), 8), :] = fv[ROWS - 1]
+        send_class(2 * b)
+
+        @pl.when(b > 0)
+        def _():
+            send_class(2 * b - 1)
+
         return 0
 
     lax.fori_loop(0, 3, local, 0)
 
-    def send_dat(i, _):
-        d = lax.rem(p + i, slabs)
-
-        @pl.when(d < solvers)
-        def _():
-            send(
-                dat_out.at[pl.ds(al(d * 24), 24), :],
-                dat_in.at[pl.ds(al(p * 24), 24), :],
-                4,
-                (d, c),
-            )
-
-        return 0
-
-    lax.fori_loop(1, slabs, send_dat, 0)
-    send(halo_out.at[pl.ds(0, 120), :], halo_in.at[pl.ds(0, 120), :], 5, (lax.rem(p + slabs - 1, slabs), c))
-    send(halo_out.at[pl.ds(120, 120), :], halo_in.at[pl.ds(120, 120), :], 6, (lax.rem(p + 1, slabs), c))
+    send(halo_out.at[pl.ds(0, 120), :], halo_in.at[pl.ds(0, 120), :], 5, (before, c))
+    send(halo_out.at[pl.ds(120, 120), :], halo_in.at[pl.ds(120, 120), :], 6, (after, c))
 
     @pl.when(is_solver)
     def _():
-        dat_in[pl.ds(al(p * 24), 24), :] = dat_out[pl.ds(al(p * 24), 24), :]
-        wait(recv_sem, 4, dat_in, (slabs - 1) * 24)
+        wait(recv_sem, 2, coef_in, (slabs - 1) * 8)
+
+        @pl.when(has_two(p))
+        def _():
+            wait(recv_sem, 8, coef_in, (slabs - 1) * 8)
+
+        for j in range(2):
+
+            def field(k):
+                return coef_in[pl.ds(j * 8 + k, slabs, stride=16), :]
+
+            gu = field(0)
+            gl = pltpu.roll(gu, 1, axis=0)
+            mm = field(1) + pltpu.roll(field(2), 1, axis=0)
+            step, s = 0, 1
+            while s < slabs:
+                rd = 1.0 / (mm + gl + gu)
+                pf = gl * pltpu.roll(rd, s, axis=0)
+                tf = gu * pltpu.roll(rd, slabs - s, axis=0)
+                at0 = ((j * 6 + step) * 2) * slabs
+                fac[pl.ds(at0, slabs), :] = pf
+                fac[pl.ds(at0 + slabs, slabs), :] = tf
+                mm = mm + pf * pltpu.roll(mm, s, axis=0) + tf * pltpu.roll(mm, slabs - s, axis=0)
+                gl = pf * pltpu.roll(gl, s, axis=0)
+                gu = tf * pltpu.roll(gu, slabs - s, axis=0)
+                step, s = step + 1, s * 2
+            fac[pl.ds((j * 6 + 5) * 2 * slabs, slabs), :] = 1.0 / (mm + gl + gu)
+
+    @pl.when(is_solver)
+    def _():
+        dat_in[pl.ds(al(p * 16), 16), :] = dat_out[pl.ds(al(p * 16), 16), :]
+        wait(recv_sem, 4, dat_in, (slabs - 1) * 16)
 
         def data(u, k):
-            return dat_in[pl.ds(u * 8 + k, slabs, stride=24), :]
+            return dat_in[pl.ds(u * 5 + k, slabs, stride=16), :]
 
         z_l = jnp.concatenate([data(u, 0) for u in range(UNITS)], axis=1)
         z_r = jnp.concatenate([data(u, 1) for u in range(UNITS)], axis=1)
@@ -490,13 +544,11 @@
             j = (UNITS * p + u) // VARS - first_tile(p)
 
             def field(k):
-                return coef_in[pl.ds(j * 16 + k, slabs, stride=32), :]
+                return coef_in[pl.ds(j * 8 + k, slabs, stride=16), :]
 
             cl, cr = c_l[:, u * 128 : u * 128 + 128], c_r[:, u * 128 : u * 128 + 128]
-            f_up = pltpu.roll(data(u, 4), slabs - 1, axis=0)
-            f_dn = pltpu.roll(data(u, 5), 1, axis=0)
-            q = data(u, 3) + field(4) * cl + field(6) * cr + field(9) * f_up
-            d = data(u, 2) + field(3) * cl + field(5) * cr + field(7) * f_dn + field(8) * f_up
+            q = data(u, 3) + field(4) * cl + field(6) * cr
+            d = data(u, 2) + field(3) * cl + field(5) * cr + pltpu.roll(data(u, 4), slabs - 1, axis=0)
             d = d + pltpu.roll(q, 1, axis=0)
             step, s = 0, 1
             while s < slabs:
@@ -572,17 +624,27 @@
     wait(send_sem, 3, pick_in, (planes - 1) * 8)
     wait(send_sem, 5, halo_in, 120)
     wait(send_sem, 6, halo_in, 120)
+    wait(send_sem, 9, side_in, 24)
+    wait(send_sem, 10, side_in, 48)
 
     @pl.when(is_solver)
     def _():
-        wait(send_sem, 2, coef_in, (solvers - 1) * 32)
-        wait(send_sem, 4, dat_in, (solvers - 1) * 24)
+        wait(send_sem, 2, coef_in, (solvers - 1) * 8)
+        wait(send_sem, 4, dat_in, (solvers - 1) * 16)
         wait(send_sem, 7, ret_out, (slabs - 1) * 16)
 
     @pl.when(jnp.logical_not(is_solver))
     def _():
-        wait(send_sem, 2, coef_in, solvers * 32)
-        wait(send_sem, 4, dat_in, solvers * 24)
+        wait(send_sem, 2, coef_in, solvers * 8)
+        wait(send_sem, 4, dat_in, solvers * 16)
+
+    @pl.when(has_two(p))
+    def _():
+        wait(send_sem, 8, coef_in, (n_two - 1) * 8)
+
+    @pl.when(jnp.logical_not(has_two(p)))
+    def _():
+        wait(send_sem, 8, coef_in, n_two * 8)
 
 
 def solution(mesh):
@@ -593,34 +655,33 @@
         pencils = state.shape[2]
         tiles = pencils // 128
         solvers = -(-(VARS * tiles) // UNITS)
-        vm = pl.BlockSpec(memory_space=pltpu.VMEM)
-        sm = pl.BlockSpec(memory_space=pltpu.SMEM)
-        out = jax.ShapeDtypeStruct(state.shape, F32)
         planes, slots = slabs // 2, cross * 2
         span = VARS * ROWS * 24
 
         def buf(rows, dtype=F32):
             return pltpu.VMEM((rows, 128), dtype)
 
-        base = base.reshape(1, -1)
-        images = pl.pallas_call(
-            functools.partial(image_kernel, tiles),
-            out_shape=jax.ShapeDtypeStruct((16, 128), F32),
-            in_specs=[sm, vm, vm, vm],
-            out_specs=vm,
+        return pl.pallas_call(
+            functools.partial(kernel, slabs, cross, tiles),
+            out_shape=(pltpu.VMEM(state.shape, F32),) * 2,
+            in_specs=[pl.BlockSpec(memory_space=pl.ANY)] * 11,
+            out_specs=(pl.BlockSpec(memory_space=pltpu.VMEM),) * 2,
             scratch_shapes=[
+                pltpu.SMEM((1, 128), F32),
+                pltpu.SMEM((1, IMAGES), I32),
+                pltpu.VMEM((2 * slabs, slabs), F32),
+                pltpu.VMEM((1, IMAGES), I32),
+                pltpu.VMEM(state.shape, F32),
+                pltpu.VMEM(face.shape, F32),
+                pltpu.VMEM(face.shape, F32),
+                pltpu.VMEM(face.shape, I32),
+                pltpu.VMEM((1, GHOSTS), I32),
+                pltpu.VMEM((1, GHOSTS), I32),
+                pltpu.VMEM((1, GHOSTS), I32),
+                pltpu.VMEM((8, IMAGES), F32),
                 buf(ROWS * (tiles + 1) * 8),
                 buf(2 * IMAGES),
                 buf(IMAGES * 8),
-            ],
-            compiler_params=pltpu.CompilerParams(vmem_limit_bytes=24 * 1024 * 1024),
-        )(base, base, state, weight)
-        return pl.pallas_call(
-            functools.partial(kernel, slabs, cross, tiles),
-            out_shape=(out, out),
-            in_specs=[sm] + [vm] * 9,
-            out_specs=(vm, vm),
-            scratch_shapes=[
                 buf(slots * 16),
                 buf(planes * 8, I32),
                 buf(planes * 8),
@@ -631,25 +692,28 @@
                 buf(span),
                 buf(ROWS * 24),
                 buf(ROWS * 24 * 6),
-                buf(384),
-                buf(slabs * 32),
+                buf(192),
+                buf(slabs * 16),
                 buf(24 * slabs),
-                buf(960),
-                buf(slabs * 24),
+                buf(72),
+                buf(72),
+                buf(640),
+                buf(slabs * 16),
                 buf(slabs * 16),
                 buf(max(640, solvers * 16)),
                 buf(240),
                 buf(240),
-                pltpu.SemaphoreType.DMA((8,)),
-                pltpu.SemaphoreType.DMA((8,)),
+                pltpu.SemaphoreType.DMA((12,)),
+                pltpu.SemaphoreType.DMA((11,)),
+                pltpu.SemaphoreType.DMA((11,)),
             ],
             compiler_params=pltpu.CompilerParams(
-                collective_id=0, has_side_effects=True, vmem_limit_bytes=40 * 1024 * 1024
+                collective_id=0, has_side_effects=True, vmem_limit_bytes=62 * 1024 * 1024
             ),
         )(
-            jnp.asarray(table), jnp.asarray(carry), images,
+            jnp.asarray(table).reshape(slabs, 1, 128), jnp.asarray(carry), base.reshape(1, -1),
             state, face, courant, cell_mask,
-            ghost_cell.reshape(1, -1), ghost_owner.reshape(1, -1), ghost_image.reshape(1, -1),
+            ghost_cell.reshape(1, -1), ghost_owner.reshape(1, -1), ghost_image.reshape(1, -1), weight,
         )
 
     flat = P(("pipe", "cross"))

time: 49.5 us -> 35 us (0.71)
  Pallas kernels: 40.7 us -> 32.5 us
  local copies, waits for them, and re-layouts: 7.71 us -> 1.73 us
    unnamed x26 -> x2, local copies, waits for them, and re-layouts: 7.71 us -> 1.73 us
    pallas_call x1, Pallas kernels: 37.4 us -> 32.5 us  [local(): pl.pallas_call(functools.partial(kernel, slabs, cross, tiles), out_shape=...]
    pallas_call x1 -> x0, Pallas kernels: 3.38 us -> none  [local(): pl.pallas_call(functools.partial(image_kernel, tiles), out_shape=jax.Shap...]
where the time goes in v2:
time: 35 us; the launch traced here: 34.9 us
  Pallas kernels  32.5 us (93%)
  local copies, waits for them, and re-layouts  1.73 us (5%)
  between operations  0.64 us (2%)
    pallas_call x1, Pallas kernels, local(): pl.pallas_call(functools.partial(kernel, slabs, cross, tiles), out_shape=...  32.5 us
    unnamed x2, local copies, waits for them, and re-layouts  1.73 us

profile of v2, /device:TPU:1, one launch (start us, length us, event | category | flops | bytes accessed | tf_op | source)
XLA Modules:
  0.0 34.9 jit_solution(7863629643218669839)
XLA Ops:
  0.6 32.5 %shard_map.122 = (f32[5,16,2304]{2,1,0:T(8,128)S(1)}, f32[5,16,2304]{2,1,0:T(8,128)S(1)}) custom-call(f32[32,1,128]{2,1,0:T(1,128)} %constant.10.tab_hbm, f32[64,32]{1,0:T(8,128)} %constant.5.clone.lam_hbm, s32[1,256]{1,0:T(1,128)} %bitcast.4, f32[5,16,2304]{2,1,0:T(8,128)} %state_hbm.1, f32[16,2304]{1,0:T(8,128)} %phi_hbm.1, f32[16,2304]{1,0:T(8,128)} %cour_hbm.1, ...), custom_call_target="tpu_custom_call" | custom-call | tf_op jit(solution)/shard_map/pallas_call | solution.py:664
  33.2 0.9 %copy.15 = f32[5,16,2304]{2,1,0:T(8,128)} copy(f32[5,16,2304]{2,1,0:T(8,128)S(1)} %get-tuple-element.2) | data formatting | bytes 1474560
  34.0 0.9 %copy.16 = f32[5,16,2304]{2,1,0:T(8,128)} copy(f32[5,16,2304]{2,1,0:T(8,128)S(1)} %get-tuple-element.3) | data formatting | bytes 1474560

commit v3 on v2

--- a/solution.py
+++ b/solution.py
@@ -13,6 +13,7 @@
 GHOSTS = 128
 IMAGES = 256
 UNITS = 3
+IMAGE_BITS = (2, 1, 0, 6, 5, 4, 3)
 REFLECT = (1.0, -1.0, -1.0, -1.0, 1.0)
 F32 = jnp.float32
 I32 = jnp.int32
@@ -96,7 +97,7 @@
 def kernel(
     slabs, cross, tiles,
     tab_hbm, lam_hbm, base_hbm, state_hbm, phi_hbm, cour_hbm, mask_hbm, gcell_hbm, gown_hbm, gimg_hbm, wts_hbm,
-    der, seg,
+    out,
     tab, base_s, lam, base_v, state, phi, cour, mask, gcell, gown, gimg, wts,
     xbuf, win, stage, tabs, req, pick_out, pick_in, gmap, fbuf, xrow, srow, crow, arow,
     coef_out, coef_in, fac, side_out, side_in, dat_out, dat_in, ret_out, ret_in, halo_out, halo_in,
@@ -119,10 +120,23 @@
         copy.start()
         return copy
 
-    got_state = fetch(0, state_hbm, state)
     got_base = fetch(1, base_hbm, base_v)
+    got_wts = fetch(3, wts_hbm, wts)
+    got_state = [fetch(0, state_hbm, state)]
     got_base_s = fetch(2, base_hbm, base_s)
-    got_wts = fetch(3, wts_hbm, wts)
+    barrier = pltpu.get_barrier_semaphore()
+
+    def greet(i, _):
+        pl.semaphore_signal(barrier, inc=1, device_id=(lax.rem(p + i, slabs), c), device_id_type=MESH)
+        return 0
+
+    lax.fori_loop(1, slabs, greet, 0)
+    for dc in range(1, cross):
+        for k in range(2):
+            pl.semaphore_signal(
+                barrier, inc=1, device_id=(yz * 2 + k, lax.rem(c + dc, cross)), device_id_type=MESH
+            )
+
     got_rest = [
         fetch(4, mask_hbm, mask),
         fetch(5, phi_hbm, phi),
@@ -150,19 +164,6 @@
 
     def al(x):
         return pl.multiple_of(x, 8)
-
-    barrier = pltpu.get_barrier_semaphore()
-
-    def greet(i, _):
-        pl.semaphore_signal(barrier, inc=1, device_id=(lax.rem(p + i, slabs), c), device_id_type=MESH)
-        return 0
-
-    lax.fori_loop(1, slabs, greet, 0)
-    for dc in range(1, cross):
-        for k in range(2):
-            pl.semaphore_signal(
-                barrier, inc=1, device_id=(yz * 2 + k, lax.rem(c + dc, cross)), device_id_type=MESH
-            )
 
     lane = lax.broadcasted_iota(I32, (8, 128), 1)
     got_base.wait()
@@ -181,7 +182,8 @@
 
     for r in range(ROWS):
         xbuf[pl.ds((r * tp + tiles) * 8, 8), :] = jnp.zeros((8, 128), F32)
-    got_state.wait()
+    for copy in got_state:
+        copy.wait()
     for rt in range(2):
         for lt in range(tiles):
             for v in range(VARS):
@@ -190,9 +192,18 @@
     got_base_s.wait()
     blocks = xbuf.reshape(ROWS * tp, 8, 128)
 
+    def merge(bit, a, b):
+        low = ((lane >> bit) & 1) == 0
+        return jnp.where(low, a, b) + pltpu.roll(jnp.where(low, b, a), 128 - (1 << bit), axis=1)
+
+    def halves(bit, vals):
+        n = len(vals) // 2
+        return [merge(bit, vals[i], vals[i + n]) for i in range(n)]
+
     def image_group(g, _):
         m0 = win[pl.ds(al(g * 8), 8), :]
         m1 = win[pl.ds(al(IMAGES + g * 8), 8), :]
+        vals = []
         for k in range(8):
             b = base_s[0, g * 8 + k]
             x = b >> 7
@@ -201,50 +212,48 @@
             inside = lane >= (b & 127)
             z0 = jnp.where(inside, blocks[off], blocks[off + 1])
             z1 = jnp.where(inside, blocks[off + tp], blocks[off + tp + 1])
-            stage[pl.ds(al((g * 8 + k) * 8), 8), :] = z0 * m0[k : k + 1, :] + z1 * m1[k : k + 1, :]
+            stage[pl.ds(al(g * 64 + k * 8), 8), :] = z0 * m0[k : k + 1, :] + z1 * m1[k : k + 1, :]
         return 0
 
-    lax.fori_loop(0, IMAGES // 8, image_group, 0)
-
-    def half_sum(h, _):
-        def node(level, i):
-            if level == 0:
-                return stage[pl.ds(al((h * 128 + i) * 8), 8), :]
-            a = node(level - 1, i)
-            b = node(level - 1, i + (128 >> level))
-            bit = level - 1
-            low = ((lane >> bit) & 1) == 0
-            return jnp.where(low, a, b) + pltpu.roll(jnp.where(low, b, a), 128 - (1 << bit), axis=1)
-
-        tabs[pl.ds(al((slot * 2 + h) * 8), 8), :] = node(7, 0)
-        return 0
-
-    lax.fori_loop(0, 2, half_sum, 0)
+    lax.fori_loop(0, IMAGES // 8, image_group, 0, unroll=4)
+    both = [[], []]
+    for g in range(IMAGES // 8):
+        vals = [stage[pl.ds(g * 64 + k * 8, 8), :] for k in range(8)]
+        for bit in range(3):
+            vals = halves(bit, vals)
+        both[g // 16].append(vals[0])
+    for bit in range(3, 7):
+        both = [halves(bit, vals) for vals in both]
+    sub = lax.broadcasted_iota(I32, (8, 128), 0)
+    second = pltpu.roll(both[1][0], VARS, axis=0)
+    tabs[pl.ds(al(yz * 16), 8), :] = jnp.where(sub < VARS, both[0][0], second)
+    tabs[pl.ds(al(yz * 16 + 8), 8), :] = second
 
     for copy in got_rest:
         copy.wait()
-    req[pl.ds(al(yz * 8), 8), :] = jnp.concatenate(
+    req[pl.ds(al(slot * 8), 8), :] = jnp.concatenate(
         [gown[...], gimg[...], jnp.zeros((6, GHOSTS), I32)], axis=0
     )
 
     pl.semaphore_wait(barrier, slabs - 1 + (cross - 1) * 2)
 
-    for dc in range(cross):
-        for dk in range(2):
-            if dc or dk:
-                send(
-                    tabs.at[pl.ds(al(slot * 16), 16), :],
-                    tabs.at[pl.ds(al(slot * 16), 16), :],
-                    0,
-                    (yz * 2 + lax.rem(core + dk, 2), lax.rem(c + dc, cross)),
-                )
-
-    def send_req(i, _):
-        mine = pl.ds(al(yz * 8), 8)
-        send(req.at[mine, :], req.at[mine, :], 1, (lax.rem(yz + i, planes) * 2 + core, c))
+    def send_table(j, _):
+        half = planes // 2
+        d = lax.rem(yz + jnp.where(j < half, half + j, planes - 1 - j), planes)
+        mine = pl.ds(al(yz * 16), 2 * VARS)
+        send(tabs.at[mine, :], tabs.at[mine, :], 0, (d * 2 + core, c))
         return 0
 
-    lax.fori_loop(1, planes, send_req, 0)
+    lax.fori_loop(0, planes - 1, send_table, 0)
+    row_peers = [
+        (yz * 2 + lax.rem(core + dk, 2), lax.rem(c + dc, cross))
+        for dc in range(cross)
+        for dk in range(2)
+        if dc or dk
+    ]
+    for dev in row_peers:
+        mine = pl.ds(al(slot * 8), 2)
+        send(req.at[mine, :], req.at[mine, :], 1, dev)
 
     for rt in range(2):
         for lt in range(tiles):
@@ -330,35 +339,6 @@
 
     n_two = sum((UNITS * d) % VARS > VARS - UNITS for d in range(solvers))
 
-    wait(recv_sem, 0, tabs, (slots - 1) * 16)
-    wait(recv_sem, 1, req, (planes - 1) * 8)
-    owner = req[pl.ds(0, planes, stride=8), :]
-    image = req[pl.ds(1, planes, stride=8), :]
-    o_c = lax.rem(owner, cross)
-    o_p = lax.div(owner, cross)
-    which = jnp.where(
-        (o_p >> 1) == yz, (o_c * 2 + (o_p & 1)) * 2 + (image >> 7), jnp.full_like(owner, -1)
-    )
-    spot7 = jnp.zeros_like(image)
-    for bit in range(7):
-        spot7 = spot7 | (((image >> bit) & 1) << (6 - bit))
-    for n in range(planes):
-        idx = jnp.broadcast_to(spot7[n : n + 1, :], (8, 128))
-        wh = jnp.broadcast_to(which[n : n + 1, :], (8, 128))
-        acc = jnp.zeros((8, 128), F32)
-        for k in range(slots * 2):
-            got = jnp.take_along_axis(tabs[pl.ds(k * 8, 8), :], idx, axis=1, mode="promise_in_bounds")
-            acc = jnp.where(wh == k, got, acc)
-        pick_out[pl.ds(n * 8, 8), :] = acc
-
-    def send_pick(i, _):
-        n = lax.rem(yz + i, planes)
-        send(pick_out.at[pl.ds(al(n * 8), 8), :], pick_in.at[pl.ds(al(yz * 8), 8), :], 3, (n * 2 + core, c))
-        return 0
-
-    lax.fori_loop(1, planes, send_pick, 0)
-    pick_in[pl.ds(al(yz * 8), 8), :] = pick_out[pl.ds(al(yz * 8), 8), :]
-
     def send_coef(i, _):
         d = lax.rem(p + i, slabs)
 
@@ -382,6 +362,43 @@
 
         return 0
 
+    wait(recv_sem, 0, tabs, (planes - 1) * 2 * VARS)
+    wait(recv_sem, 1, req, (slots - 1) * 2)
+    owner = req[pl.ds(0, slots, stride=8), :]
+    image = req[pl.ds(1, slots, stride=8), :]
+    o_c = lax.rem(owner, cross)
+    o_p = lax.div(owner, cross)
+    held = jnp.logical_and(o_c == c, (o_p & 1) == core)
+    which = jnp.where(held, (o_p >> 1) * 2 + (image >> 7), jnp.full_like(owner, -1))
+    spot7 = jnp.zeros_like(image)
+    for bit in range(7):
+        spot7 = spot7 | (((image >> bit) & 1) << IMAGE_BITS[bit])
+    tables = []
+    for k in range(planes):
+        first, second = tabs[pl.ds(k * 16, 8), :], tabs[pl.ds(k * 16 + 8, 8), :]
+        back = 8 - VARS
+        tables += [
+            first,
+            jnp.where(sub < back, pltpu.roll(first, back, axis=0), pltpu.roll(second, back, axis=0)),
+        ]
+    for n in range(slots):
+        idx = jnp.broadcast_to(spot7[n : n + 1, :], (8, 128))
+        wh = jnp.broadcast_to(which[n : n + 1, :], (8, 128))
+        acc = jnp.zeros((8, 128), F32)
+        for k in range(planes * 2):
+            got = jnp.take_along_axis(tables[k], idx, axis=1, mode="promise_in_bounds")
+            acc = jnp.where(wh == k, got, acc)
+        pick_out[pl.ds(n * 8, 8), :] = acc
+
+    for dev in row_peers:
+        send(
+            pick_out.at[pl.ds(al((dev[1] * 2 + lax.rem(dev[0], 2)) * 8), VARS), :],
+            pick_in.at[pl.ds(al(slot * 8), VARS), :],
+            3,
+            dev,
+        )
+    pick_in[pl.ds(al(slot * 8), 8), :] = pick_out[pl.ds(al(slot * 8), 8), :]
+
     send(side_out.at[pl.ds(0, 24), :], side_in.at[pl.ds(0, 24), :], 9, (before, c))
     send(side_out.at[pl.ds(24, 48), :], side_in.at[pl.ds(24, 48), :], 10, (after, c))
     lax.fori_loop(1, slabs, send_coef, 0)
@@ -390,9 +407,9 @@
     def _():
         coef_in[pl.ds(al(p * 16), 16), :] = coef_out[pl.ds(al(first_tile(p) * 8), 16), :]
 
-    wait(recv_sem, 3, pick_in, (planes - 1) * 8)
+    wait(recv_sem, 3, pick_in, (slots - 1) * VARS)
     ghost = pick_in[pl.ds(0, 8), :]
-    for n in range(1, planes):
+    for n in range(1, slots):
         ghost = ghost + pick_in[pl.ds(n * 8, 8), :]
     ghost = [jnp.broadcast_to(REFLECT[v] * ghost[v : v + 1, :], (8, 128)) for v in range(VARS)]
 
@@ -563,16 +580,16 @@
 
         def send_ret(i, _):
             d = lax.rem(p + i, slabs)
-            send(ret_out.at[pl.ds(al(d * 16), 16), :], ret_in.at[pl.ds(al(p * 16), 16), :], 7, (d, c))
+            send(ret_out.at[pl.ds(al(d * 16), 12), :], ret_in.at[pl.ds(al(p * 16), 12), :], 7, (d, c))
             return 0
 
         lax.fori_loop(1, slabs, send_ret, 0)
         ret_in[pl.ds(al(p * 16), 16), :] = ret_out[pl.ds(al(p * 16), 16), :]
-        wait(recv_sem, 7, ret_in, (solvers - 1) * 16)
+        wait(recv_sem, 7, ret_in, (solvers - 1) * 12)
 
     @pl.when(jnp.logical_not(is_solver))
     def _():
-        wait(recv_sem, 7, ret_in, solvers * 16)
+        wait(recv_sem, 7, ret_in, solvers * 12)
 
     wait(recv_sem, 5, halo_in, 120)
     wait(recv_sem, 6, halo_in, 120)
@@ -616,12 +633,12 @@
         for rt in range(2):
             for lt in range(tiles):
                 src = pl.ds((v * ROWS + rt * 8) * 24 + (lt % 3) * 8 + lt // 3, 8, stride=24)
-                der[v, pl.ds(rt * 8, 8), pl.ds(lt * 128, 128)] = xrow[src, :]
-                seg[v, pl.ds(rt * 8, 8), pl.ds(lt * 128, 128)] = srow[src, :]
-
-    wait(send_sem, 0, tabs, (slots - 1) * 16)
-    wait(send_sem, 1, req, (planes - 1) * 8)
-    wait(send_sem, 3, pick_in, (planes - 1) * 8)
+                out[0, v, pl.ds(rt * 8, 8), pl.ds(lt * 128, 128)] = xrow[src, :]
+                out[1, v, pl.ds(rt * 8, 8), pl.ds(lt * 128, 128)] = srow[src, :]
+
+    wait(send_sem, 0, tabs, (planes - 1) * 2 * VARS)
+    wait(send_sem, 1, req, (slots - 1) * 2)
+    wait(send_sem, 3, pick_in, (slots - 1) * VARS)
     wait(send_sem, 5, halo_in, 120)
     wait(send_sem, 6, halo_in, 120)
     wait(send_sem, 9, side_in, 24)
@@ -631,7 +648,7 @@
     def _():
         wait(send_sem, 2, coef_in, (solvers - 1) * 8)
         wait(send_sem, 4, dat_in, (solvers - 1) * 16)
-        wait(send_sem, 7, ret_out, (slabs - 1) * 16)
+        wait(send_sem, 7, ret_out, (slabs - 1) * 12)
 
     @pl.when(jnp.logical_not(is_solver))
     def _():
@@ -661,11 +678,11 @@
         def buf(rows, dtype=F32):
             return pltpu.VMEM((rows, 128), dtype)
 
-        return pl.pallas_call(
+        out = pl.pallas_call(
             functools.partial(kernel, slabs, cross, tiles),
-            out_shape=(pltpu.VMEM(state.shape, F32),) * 2,
+            out_shape=pltpu.VMEM((2, *state.shape), F32),
             in_specs=[pl.BlockSpec(memory_space=pl.ANY)] * 11,
-            out_specs=(pl.BlockSpec(memory_space=pltpu.VMEM),) * 2,
+            out_specs=pl.BlockSpec(memory_space=pltpu.VMEM),
             scratch_shapes=[
                 pltpu.SMEM((1, 128), F32),
                 pltpu.SMEM((1, IMAGES), I32),
@@ -682,10 +699,10 @@
                 buf(ROWS * (tiles + 1) * 8),
                 buf(2 * IMAGES),
                 buf(IMAGES * 8),
-                buf(slots * 16),
-                buf(planes * 8, I32),
-                buf(planes * 8),
-                buf(planes * 8),
+                buf(planes * 16),
+                buf(slots * 8, I32),
+                buf(slots * 8),
+                buf(slots * 8),
                 buf(ROWS * 24, I32),
                 buf(span),
                 buf(span),
@@ -703,7 +720,7 @@
                 buf(max(640, solvers * 16)),
                 buf(240),
                 buf(240),
-                pltpu.SemaphoreType.DMA((12,)),
+                pltpu.SemaphoreType.DMA((16,)),
                 pltpu.SemaphoreType.DMA((11,)),
                 pltpu.SemaphoreType.DMA((11,)),
             ],
@@ -715,6 +732,7 @@
             state, face, courant, cell_mask,
             ghost_cell.reshape(1, -1), ghost_owner.reshape(1, -1), ghost_image.reshape(1, -1), weight,
         )
+        return out[0], out[1]
 
     flat = P(("pipe", "cross"))
     slab = P("pipe", "cross")

time: 35 us -> 33.4 us (0.954)
  Pallas kernels: 32.5 us -> 31.4 us
  local copies, waits for them, and re-layouts: 1.73 us -> 1.22 us
    unnamed x2 -> x0, local copies, waits for them, and re-layouts: 1.73 us -> none
    squeeze x0 -> x1, local copies, waits for them, and re-layouts: none -> 1.22 us  [local(): return (out[0], out[1])]
    pallas_call x1, Pallas kernels: 32.5 us -> 31.4 us  [local(): pl.pallas_call(functools.partial(kernel, slabs, cross, tiles), out_shape=...]
where the time goes in v3:
time: 33.4 us; the launch traced here: 33.3 us
  Pallas kernels  31.4 us (94%)
  local copies, waits for them, and re-layouts  1.22 us (4%)
  between operations  0.64 us (2%)
    pallas_call x1, Pallas kernels, local(): pl.pallas_call(functools.partial(kernel, slabs, cross, tiles), out_shape=...  31.4 us
    squeeze x1, local copies, waits for them, and re-layouts, local(): return (out[0], out[1])  1.22 us

profile of v3, /device:TPU:1, one launch (start us, length us, event | category | flops | bytes accessed | tf_op | source)
XLA Modules:
  0.0 33.3 jit_solution(12693848782213311473)
XLA Ops:
  0.6 31.4 %shard_map.122 = f32[2,5,16,2304]{3,2,1,0:T(8,128)S(1)} custom-call(f32[32,1,128]{2,1,0:T(1,128)} %constant.10.tab_hbm, f32[64,32]{1,0:T(8,128)} %constant.5.clone.lam_hbm, s32[1,256]{1,0:T(1,128)} %bitcast.8, f32[5,16,2304]{2,1,0:T(8,128)} %state_hbm.1, f32[16,2304]{1,0:T(8,128)} %phi_hbm.1, f32[16,2304]{1,0:T(8,128)} %cour_hbm.1, s32[16,2304]{1,0:T(8,128)} %mask_hbm.1, ...), custom_call_target="tpu_custom_call" | custom-call | tf_op jit(solution)/shard_map/pallas_call | solution.py:681
  32.1 1.2 %slice_bitcast_fusion = (f32[5,16,2304]{2,1,0:T(8,128)}, f32[5,16,2304]{2,1,0:T(8,128)}) fusion(f32[2,5,16,2304]{3,2,1,0:T(8,128)S(1)} %shard_map.122), kind=kLoop, calls=%fused_computation | loop fusion | bytes 2949120 | tf_op jit(solution)/shard_map/squeeze | solution.py:735

commit v4 on v3

--- a/solution.py
+++ b/solution.py
@@ -511,9 +511,6 @@
 
     lax.fori_loop(0, 3, local, 0)
 
-    send(halo_out.at[pl.ds(0, 120), :], halo_in.at[pl.ds(0, 120), :], 5, (before, c))
-    send(halo_out.at[pl.ds(120, 120), :], halo_in.at[pl.ds(120, 120), :], 6, (after, c))
-
     @pl.when(is_solver)
     def _():
         wait(recv_sem, 2, coef_in, (slabs - 1) * 8)
@@ -544,6 +541,9 @@
                 step, s = step + 1, s * 2
             fac[pl.ds((j * 6 + 5) * 2 * slabs, slabs), :] = 1.0 / (mm + gl + gu)
 
+    send(halo_out.at[pl.ds(0, 120), :], halo_in.at[pl.ds(0, 120), :], 5, (before, c))
+    send(halo_out.at[pl.ds(120, 120), :], halo_in.at[pl.ds(120, 120), :], 6, (after, c))
+
     @pl.when(is_solver)
     def _():
         dat_in[pl.ds(al(p * 16), 16), :] = dat_out[pl.ds(al(p * 16), 16), :]
@@ -598,6 +598,9 @@
         def at(row):
             return pl.ds(al(row * 24 + b * 8), 8)
 
+        def natural(which, v, i):
+            return pl.ds((((which * VARS + v) * 2 + i // 8) * tiles + b) * 8 + i % 8, tiles // 3, stride=24)
+
         for v in range(VARS):
             w = 5 * b + v
 
@@ -614,7 +617,7 @@
                     xi = xi + tv(T_DL) * below
                 if i == ROWS - 1:
                     xi = xi + tv(T_DR) * above
-                xrow[at(v * ROWS + i), :] = xi
+                out[natural(0, v, i), :] = xi[: tiles // 3]
                 if i:
                     rhs = fbuf[at(v * ROWS + i), :] - crow[at(i), :] * xi
                     run = rhs if run is None else rhs + arow[at(16 + E + i - 1), :] * run
@@ -624,18 +627,11 @@
             y = t1
             for i in range(ROWS - 1, 0, -1):
                 y = srow[at(v * ROWS + i), :] + arow[at(16 + E + i), :] * y
-                srow[at(v * ROWS + i), :] = y
-            srow[at(v * ROWS), :] = t0
+                out[natural(1, v, i), :] = y[: tiles // 3]
+            out[natural(1, v, 0), :] = t0[: tiles // 3]
         return 0
 
     lax.fori_loop(0, 3, finish, 0)
-    for v in range(VARS):
-        for rt in range(2):
-            for lt in range(tiles):
-                src = pl.ds((v * ROWS + rt * 8) * 24 + (lt % 3) * 8 + lt // 3, 8, stride=24)
-                out[0, v, pl.ds(rt * 8, 8), pl.ds(lt * 128, 128)] = xrow[src, :]
-                out[1, v, pl.ds(rt * 8, 8), pl.ds(lt * 128, 128)] = srow[src, :]
-
     wait(send_sem, 0, tabs, (planes - 1) * 2 * VARS)
     wait(send_sem, 1, req, (slots - 1) * 2)
     wait(send_sem, 3, pick_in, (slots - 1) * VARS)
@@ -680,7 +676,7 @@
 
         out = pl.pallas_call(
             functools.partial(kernel, slabs, cross, tiles),
-            out_shape=pltpu.VMEM((2, *state.shape), F32),
+            out_shape=pltpu.VMEM((2 * VARS * ROWS * tiles, 128), F32),
             in_specs=[pl.BlockSpec(memory_space=pl.ANY)] * 11,
             out_specs=pl.BlockSpec(memory_space=pltpu.VMEM),
             scratch_shapes=[
@@ -732,6 +728,7 @@
             state, face, courant, cell_mask,
             ghost_cell.reshape(1, -1), ghost_owner.reshape(1, -1), ghost_image.reshape(1, -1), weight,
         )
+        out = out.reshape(2, VARS, 2, tiles, 8, 128).transpose(0, 1, 2, 4, 3, 5).reshape(2, *state.shape)
         return out[0], out[1]
 
     flat = P(("pipe", "cross"))

time: 33.4 us -> 33.2 us (level)
  no operation moved by 1% of the time
where the time goes in v4:
time: 33.2 us; the launch traced here: 33.1 us
  Pallas kernels  31.2 us (94%)
  local copies, waits for them, and re-layouts  1.22 us (4%)
  between operations  0.64 us (2%)
    pallas_call x1, Pallas kernels, local(): pl.pallas_call(functools.partial(kernel, slabs, cross, tiles), out_shape=...  31.2 us
    squeeze x1, local copies, waits for them, and re-layouts, local(): return (out[0], out[1])  1.22 us

profile of v4, /device:TPU:1, one launch (start us, length us, event | category | flops | bytes accessed | tf_op | source)
XLA Modules:
  0.0 33.1 jit_solution(6903376062156549959)
XLA Ops:
  0.6 31.2 %shard_map.122 = f32[2880,128]{1,0:T(8,128)S(1)} custom-call(f32[32,1,128]{2,1,0:T(1,128)} %constant.10.tab_hbm, f32[64,32]{1,0:T(8,128)} %constant.5.clone.lam_hbm, s32[1,256]{1,0:T(1,128)} %bitcast.12, f32[5,16,2304]{2,1,0:T(8,128)} %state_hbm.1, f32[16,2304]{1,0:T(8,128)} %phi_hbm.1, f32[16,2304]{1,0:T(8,128)} %cour_hbm.1, s32[16,2304]{1,0:T(8,128)} %mask_hbm.1, ...), custom_call_target="tpu_custom_call" | custom-call | tf_op jit(solution)/shard_map/pallas_call | solution.py:677
  31.9 1.2 %slice_bitcast_fusion = (f32[5,16,2304]{2,1,0:T(8,128)}, f32[5,16,2304]{2,1,0:T(8,128)}) fusion(f32[2,5,2,8,18,128]{5,3,4,2,1,0:T(8,128)S(1)} %bitcast.11), kind=kLoop, calls=%fused_computation | loop fusion | bytes 2949120 | tf_op jit(solution)/shard_map/squeeze | solution.py:732

commit v5 on v4

--- a/solution.py
+++ b/solution.py
@@ -97,9 +97,9 @@
 def kernel(
     slabs, cross, tiles,
     tab_hbm, lam_hbm, base_hbm, state_hbm, phi_hbm, cour_hbm, mask_hbm, gcell_hbm, gown_hbm, gimg_hbm, wts_hbm,
-    out,
+    fbuf, xrow, crow, arow, returns, ends, scale,
     tab, base_s, lam, base_v, state, phi, cour, mask, gcell, gown, gimg, wts,
-    xbuf, win, stage, tabs, req, pick_out, pick_in, gmap, fbuf, xrow, srow, crow, arow,
+    xbuf, win, stage, tabs, req, pick_out, pick_in, gmap, srow,
     coef_out, coef_in, fac, side_out, side_in, dat_out, dat_in, ret_out, ret_in, halo_out, halo_in,
     in_sem, send_sem, recv_sem,
 ):
@@ -435,6 +435,11 @@
             return 0
 
         lax.fori_loop(0, tiles // 3, one, 0)
+
+    for k in range(2 * ROWS):
+        scale[pl.ds(k, 1), :] = jnp.full((1, 128), tv(T_U + k), F32)
+    for k in range(2):
+        scale[pl.ds(2 * ROWS + k, 1), :] = jnp.full((1, 128), tv(T_DL + k), F32)
 
     def local(b, _):
         def at(row):
@@ -594,44 +599,9 @@
     wait(recv_sem, 5, halo_in, 120)
     wait(recv_sem, 6, halo_in, 120)
 
-    def finish(b, _):
-        def at(row):
-            return pl.ds(al(row * 24 + b * 8), 8)
-
-        def natural(which, v, i):
-            return pl.ds((((which * VARS + v) * 2 + i // 8) * tiles + b) * 8 + i % 8, tiles // 3, stride=24)
-
-        for v in range(VARS):
-            w = 5 * b + v
-
-            def back(k):
-                return ret_in[pl.ds((w // 3) * 16 + (w % 3) * 4 + k, 8, stride=80), :]
-
-            left_c, right_c, t0, t1 = back(0), back(1), back(2), back(3)
-            above = halo_in[at(v), :]
-            below = halo_in[at(5 + v), :]
-            run = None
-            for i in range(ROWS):
-                xi = xrow[at(v * ROWS + i), :] + tv(T_U + i) * left_c + tv(T_V + i) * right_c
-                if i == 0:
-                    xi = xi + tv(T_DL) * below
-                if i == ROWS - 1:
-                    xi = xi + tv(T_DR) * above
-                out[natural(0, v, i), :] = xi[: tiles // 3]
-                if i:
-                    rhs = fbuf[at(v * ROWS + i), :] - crow[at(i), :] * xi
-                    run = rhs if run is None else rhs + arow[at(16 + E + i - 1), :] * run
-                    srow[at(v * ROWS + i), :] = (
-                        arow[at(16 + RD + i), :] * run + arow[at(16 + H + i), :] * t0
-                    )
-            y = t1
-            for i in range(ROWS - 1, 0, -1):
-                y = srow[at(v * ROWS + i), :] + arow[at(16 + E + i), :] * y
-                out[natural(1, v, i), :] = y[: tiles // 3]
-            out[natural(1, v, 0), :] = t0[: tiles // 3]
-        return 0
-
-    lax.fori_loop(0, 3, finish, 0)
+    returns[...] = ret_in[...]
+    ends[...] = halo_in[...]
+
     wait(send_sem, 0, tabs, (planes - 1) * 2 * VARS)
     wait(send_sem, 1, req, (slots - 1) * 2)
     wait(send_sem, 3, pick_in, (slots - 1) * VARS)
@@ -660,6 +630,61 @@
         wait(send_sem, 8, coef_in, n_two * 8)
 
 
+def finish(tiles, fbuf, xrow, crow, arow, returns, ends, scale, der, seg, x_out, y_out, srow, sem):
+    E, H, RD = 16, 32, 48
+
+    def one(v):
+        def third(b, _):
+            def at(row):
+                return pl.ds(pl.multiple_of(row * 24 + b * 8, 8), 8)
+
+            def natural(i):
+                return pl.ds(((v * 2 + i // 8) * tiles + b) * 8 + i % 8, tiles // 3, stride=24)
+
+            def const(k):
+                return scale[pl.ds(k, 1), :]
+
+            w = 5 * b + v
+
+            def given(k):
+                return returns[pl.ds((w // 3) * 16 + (w % 3) * 4 + k, 8, stride=80), :]
+
+            left_c, right_c, t0, t1 = given(0), given(1), given(2), given(3)
+            above = ends[at(v), :]
+            below = ends[at(5 + v), :]
+            run = None
+            for i in range(ROWS):
+                xi = xrow[at(v * ROWS + i), :] + const(i) * left_c + const(ROWS + i) * right_c
+                if i == 0:
+                    xi = xi + const(2 * ROWS) * below
+                if i == ROWS - 1:
+                    xi = xi + const(2 * ROWS + 1) * above
+                x_out[natural(i), :] = xi[: tiles // 3]
+                if i:
+                    rhs = fbuf[at(v * ROWS + i), :] - crow[at(i), :] * xi
+                    run = rhs if run is None else rhs + arow[at(E + i - 1), :] * run
+                    srow[at(i), :] = arow[at(RD + i), :] * run + arow[at(H + i), :] * t0
+            y = t1
+            for i in range(ROWS - 1, 0, -1):
+                y = srow[at(i), :] + arow[at(E + i), :] * y
+                y_out[natural(i), :] = y[: tiles // 3]
+            y_out[natural(0), :] = t0[: tiles // 3]
+            return 0
+
+        lax.fori_loop(0, 3, third, 0, unroll=3)
+
+    rows = ROWS * tiles
+    copies = []
+    for v in range(VARS):
+        one(v)
+        part = pl.ds(v * rows, rows)
+        for k, (src, dst) in enumerate(((x_out, der), (y_out, seg))):
+            copies.append(pltpu.make_async_copy(src.at[part, :], dst.at[part, :], sem.at[k, v]))
+            copies[-1].start()
+    for copy in copies:
+        copy.wait()
+
+
 def solution(mesh):
     slabs, cross = mesh.shape["pipe"], mesh.shape["cross"]
     table, carry = derivative_constants(slabs)
@@ -674,11 +699,13 @@
         def buf(rows, dtype=F32):
             return pltpu.VMEM((rows, 128), dtype)
 
-        out = pl.pallas_call(
+        parts = pl.pallas_call(
             functools.partial(kernel, slabs, cross, tiles),
-            out_shape=pltpu.VMEM((2 * VARS * ROWS * tiles, 128), F32),
+            out_shape=tuple(
+                buf(n) for n in (span, span, ROWS * 24, ROWS * 24 * 6, max(640, solvers * 16), 240, 2 * ROWS + 8)
+            ),
             in_specs=[pl.BlockSpec(memory_space=pl.ANY)] * 11,
-            out_specs=pl.BlockSpec(memory_space=pltpu.VMEM),
+            out_specs=(pl.BlockSpec(memory_space=pltpu.VMEM),) * 7,
             scratch_shapes=[
                 pltpu.SMEM((1, 128), F32),
                 pltpu.SMEM((1, IMAGES), I32),
@@ -701,10 +728,6 @@
                 buf(slots * 8),
                 buf(ROWS * 24, I32),
                 buf(span),
-                buf(span),
-                buf(span),
-                buf(ROWS * 24),
-                buf(ROWS * 24 * 6),
                 buf(192),
                 buf(slabs * 16),
                 buf(24 * slabs),
@@ -721,15 +744,25 @@
                 pltpu.SemaphoreType.DMA((11,)),
             ],
             compiler_params=pltpu.CompilerParams(
-                collective_id=0, has_side_effects=True, vmem_limit_bytes=62 * 1024 * 1024
+                collective_id=0, has_side_effects=True, vmem_limit_bytes=59 * 1024 * 1024
             ),
         )(
             jnp.asarray(table).reshape(slabs, 1, 128), jnp.asarray(carry), base.reshape(1, -1),
             state, face, courant, cell_mask,
             ghost_cell.reshape(1, -1), ghost_owner.reshape(1, -1), ghost_image.reshape(1, -1), weight,
         )
-        out = out.reshape(2, VARS, 2, tiles, 8, 128).transpose(0, 1, 2, 4, 3, 5).reshape(2, *state.shape)
-        return out[0], out[1]
+        rows = VARS * ROWS * tiles
+        results = pl.pallas_call(
+            functools.partial(finish, tiles),
+            out_shape=(jax.ShapeDtypeStruct((rows, 128), F32),) * 2,
+            in_specs=[pl.BlockSpec(memory_space=pltpu.VMEM)] * 7,
+            out_specs=(pl.BlockSpec(memory_space=pl.ANY),) * 2,
+            scratch_shapes=[buf(rows), buf(rows), buf(ROWS * 24), pltpu.SemaphoreType.DMA((2, VARS))],
+            compiler_params=pltpu.CompilerParams(vmem_limit_bytes=3 * 1024 * 1024),
+        )(*parts)
+        return tuple(
+            x.reshape(VARS, 2, tiles, 8, 128).transpose(0, 1, 3, 2, 4).reshape(state.shape) for x in results
+        )
 
     flat = P(("pipe", "cross"))
     slab = P("pipe", "cross")

time: 33.2 us -> 32.8 us (0.988)
  local copies, waits for them, and re-layouts: 1.22 us -> 0 us
  Pallas kernels: 31.2 us -> 32.1 us
    pallas_call x0 -> x1, Pallas kernels: none -> 1.41 us  [local(): pl.pallas_call(functools.partial(finish, tiles), out_shape=(jax.ShapeDtyp...]
    squeeze x1 -> x0, local copies, waits for them, and re-layouts: 1.22 us -> none  [local(): return (out[0], out[1])]
    pallas_call x1, Pallas kernels: 31.2 us -> 30.7 us  [local(): pl.pallas_call(functools.partial(kernel, slabs, cross, tiles), out_shape=...]
where the time goes in v5:
time: 32.8 us; the launch traced here: 32.7 us
  Pallas kernels  32.1 us (98%)
  between operations  0.64 us (2%)
    pallas_call x1, Pallas kernels, local(): pl.pallas_call(functools.partial(kernel, slabs, cross, tiles), out_shape=...  30.7 us
    pallas_call x1, Pallas kernels, local(): pl.pallas_call(functools.partial(finish, tiles), out_shape=(jax.ShapeDtyp...  1.41 us

profile of v5, /device:TPU:1, one launch (start us, length us, event | category | flops | bytes accessed | tf_op | source)
XLA Modules:
  0.0 32.7 jit_solution(2480673343047216906)
XLA Ops:
  0.6 30.7 %shard_map.122 = (f32[1920,128]{1,0:T(8,128)S(1)}, f32[1920,128]{1,0:T(8,128)S(1)}, f32[384,128]{1,0:T(8,128)S(1)}, f32[2304,128]{1,0:T(8,128)S(1)}, f32[640,128...) custom-call(f32[32,1,128]{2,1,0:T(1,128)} %constant.10.tab_hbm, f32[64,32]{1,0:T(8,128)} %constant.5.clone.lam_hbm, ...), custom_call_target="tpu_custom_call" | custom-call | tf_op jit(solution)/shard_map/pallas_call | solution.py:702
  31.3 1.4 %shard_map.123 = (f32[1440,128]{1,0:T(8,128)}, f32[1440,128]{1,0:T(8,128)}) custom-call(f32[1920,128]{1,0:T(8,128)S(1)} %get-tuple-element.11.fbuf, f32[1920,128]{1,0:T(8,128)S(1)} %get-tuple-element.12.xrow, f32[384,128]{1,0:T(8,128)S(1)} %get-tuple-element.13.crow, f32[2304,128]{1,0:T(8,128)S(1)} %get-tuple-element.14.arow, ...), custom_call_target="tpu_custom_call" | custom-call | tf_op jit(solution)/shard_map/pallas_call | solution.py:755

commit v6 on v5

--- a/solution.py
+++ b/solution.py
@@ -130,7 +130,7 @@
         pl.semaphore_signal(barrier, inc=1, device_id=(lax.rem(p + i, slabs), c), device_id_type=MESH)
         return 0
 
-    lax.fori_loop(1, slabs, greet, 0)
+    lax.fori_loop(1, slabs, greet, 0, unroll=True)
     for dc in range(1, cross):
         for k in range(2):
             pl.semaphore_signal(
@@ -244,7 +244,7 @@
         send(tabs.at[mine, :], tabs.at[mine, :], 0, (d * 2 + core, c))
         return 0
 
-    lax.fori_loop(0, planes - 1, send_table, 0)
+    lax.fori_loop(0, planes - 1, send_table, 0, unroll=True)
     row_peers = [
         (yz * 2 + lax.rem(core + dk, 2), lax.rem(c + dc, cross))
         for dc in range(cross)
@@ -434,7 +434,7 @@
 
             return 0
 
-        lax.fori_loop(0, tiles // 3, one, 0)
+        lax.fori_loop(0, tiles // 3, one, 0, unroll=True)
 
     for k in range(2 * ROWS):
         scale[pl.ds(k, 1), :] = jnp.full((1, 128), tv(T_U + k), F32)
@@ -514,7 +514,7 @@
 
         return 0
 
-    lax.fori_loop(0, 3, local, 0)
+    lax.fori_loop(0, 3, local, 0, unroll=3)
 
     @pl.when(is_solver)
     def _():
@@ -588,7 +588,7 @@
             send(ret_out.at[pl.ds(al(d * 16), 12), :], ret_in.at[pl.ds(al(p * 16), 12), :], 7, (d, c))
             return 0
 
-        lax.fori_loop(1, slabs, send_ret, 0)
+        lax.fori_loop(1, slabs, send_ret, 0, unroll=4)
         ret_in[pl.ds(al(p * 16), 16), :] = ret_out[pl.ds(al(p * 16), 16), :]
         wait(recv_sem, 7, ret_in, (solvers - 1) * 12)
 

time: 32.8 us -> 32.5 us (level)
  no operation moved by 1% of the time
where the time goes in v6:
time: 32.5 us; the launch traced here: 32.4 us
  Pallas kernels  31.8 us (98%)
  between operations  0.64 us (2%)
    pallas_call x1, Pallas kernels, local(): pl.pallas_call(functools.partial(kernel, slabs, cross, tiles), out_shape=...  30.4 us
    pallas_call x1, Pallas kernels, local(): pl.pallas_call(functools.partial(finish, tiles), out_shape=(jax.ShapeDtyp...  1.41 us

profile of v6, /device:TPU:1, one launch (start us, length us, event | category | flops | bytes accessed | tf_op | source)
XLA Modules:
  0.0 32.4 jit_solution(17183597781560811781)
XLA Ops:
  0.6 30.4 %shard_map.122 = (f32[1920,128]{1,0:T(8,128)S(1)}, f32[1920,128]{1,0:T(8,128)S(1)}, f32[384,128]{1,0:T(8,128)S(1)}, f32[2304,128]{1,0:T(8,128)S(1)}, f32[640,128...) custom-call(f32[32,1,128]{2,1,0:T(1,128)} %constant.10.tab_hbm, f32[64,32]{1,0:T(8,128)} %constant.5.clone.lam_hbm, ...), custom_call_target="tpu_custom_call" | custom-call | tf_op jit(solution)/shard_map/pallas_call | solution.py:702
  31.0 1.4 %shard_map.123 = (f32[1440,128]{1,0:T(8,128)}, f32[1440,128]{1,0:T(8,128)}) custom-call(f32[1920,128]{1,0:T(8,128)S(1)} %get-tuple-element.11.fbuf, f32[1920,128]{1,0:T(8,128)S(1)} %get-tuple-element.12.xrow, f32[384,128]{1,0:T(8,128)S(1)} %get-tuple-element.13.crow, f32[2304,128]{1,0:T(8,128)S(1)} %get-tuple-element.14.arow, ...), custom_call_target="tpu_custom_call" | custom-call | tf_op jit(solution)/shard_map/pallas_call | solution.py:755

commit v7 on v6

--- a/solution.py
+++ b/solution.py
@@ -588,7 +588,7 @@
             send(ret_out.at[pl.ds(al(d * 16), 12), :], ret_in.at[pl.ds(al(p * 16), 12), :], 7, (d, c))
             return 0
 
-        lax.fori_loop(1, slabs, send_ret, 0, unroll=4)
+        lax.fori_loop(1, slabs, send_ret, 0, unroll=True)
         ret_in[pl.ds(al(p * 16), 16), :] = ret_out[pl.ds(al(p * 16), 16), :]
         wait(recv_sem, 7, ret_in, (solvers - 1) * 12)
 

time: 32.5 us -> 32.5 us (level)
  no operation moved by 1% of the time
where the time goes in v7:
time: 32.5 us; the launch traced here: 32.4 us
  Pallas kernels  31.8 us (98%)
  between operations  0.64 us (2%)
    pallas_call x1, Pallas kernels, local(): pl.pallas_call(functools.partial(kernel, slabs, cross, tiles), out_shape=...  30.4 us
    pallas_call x1, Pallas kernels, local(): pl.pallas_call(functools.partial(finish, tiles), out_shape=(jax.ShapeDtyp...  1.41 us

profile of v7, /device:TPU:1, one launch (start us, length us, event | category | flops | bytes accessed | tf_op | source)
XLA Modules:
  0.0 32.4 jit_solution(5500908096289797856)
XLA Ops:
  0.6 30.4 %shard_map.122 = (f32[1920,128]{1,0:T(8,128)S(1)}, f32[1920,128]{1,0:T(8,128)S(1)}, f32[384,128]{1,0:T(8,128)S(1)}, f32[2304,128]{1,0:T(8,128)S(1)}, f32[640,128...) custom-call(f32[32,1,128]{2,1,0:T(1,128)} %constant.10.tab_hbm, f32[64,32]{1,0:T(8,128)} %constant.5.clone.lam_hbm, ...), custom_call_target="tpu_custom_call" | custom-call | tf_op jit(solution)/shard_map/pallas_call | solution.py:702
  31.0 1.4 %shard_map.123 = (f32[1440,128]{1,0:T(8,128)}, f32[1440,128]{1,0:T(8,128)}) custom-call(f32[1920,128]{1,0:T(8,128)S(1)} %get-tuple-element.11.fbuf, f32[1920,128]{1,0:T(8,128)S(1)} %get-tuple-element.12.xrow, f32[384,128]{1,0:T(8,128)S(1)} %get-tuple-element.13.crow, f32[2304,128]{1,0:T(8,128)S(1)} %get-tuple-element.14.arow, ...), custom_call_target="tpu_custom_call" | custom-call | tf_op jit(solution)/shard_map/pallas_call | solution.py:755
